TPU v7x, 256 devices: a whole 4x4x8 slice. The times are simulated.
256 devices in a mesh: img: 32 (over z, x_lo, core), row: 8 (over x_hi, y).
Axes of the slice: x: 4 (x_hi: 2, x_lo: 2; x = x_hi * 2 + x_lo), y: 4, z: 8, core: 2. Of those that a mesh axis runs over, the one named last changes fastest.
Arguments:
- llm_hidden: bfloat16 [16384, 6656], P('img', 'row'), may hold values from -96 to 96
- slot_start: int32 [32], P('img'), may hold values from 0 to 448
- image_group: int32 [32], replicated, may hold values from 0 to 31, each once
- timesteps: int32 [32], P('img'), may hold values from 0 to 999
- latents: float32 [32, 4, 64, 128], P('img', None, 'row'), may hold values from -6 to 6
- noise: float32 [32, 4, 64, 128], P('img', None, 'row'), may hold values from -6 to 6
- kv_weight: bfloat16 [6656, 640], P('row'), may hold values from -0.078125 to 0.078125
- in_weight: bfloat16 [3, 3, 320, 4], replicated, may hold values from -1 to 1
- res_weight: bfloat16 [3, 3, 320, 320], replicated, may hold values from -0.109375 to 0.109375
- query_weight: bfloat16 [320, 320], replicated, may hold values from -0.3125 to 0.3125
- out_weight: bfloat16 [320, 320], replicated, may hold values from -0.3125 to 0.3125
- cotangent: bfloat16 [32, 320, 64, 128], P('img', None, 'row'), may hold values from -6 to 6
Outputs:
- block_out: bfloat16 [32, 320, 64, 128], P('img', None, 'row')
- grad_hidden: bfloat16 [16384, 6656], P('img', 'row')
- grad_kv_weight: bfloat16 [6656, 640], P('row')
- grad_res_weight: bfloat16 [3, 3, 320, 320], replicated
- grad_query_weight: bfloat16 [320, 320], replicated
- grad_out_weight: bfloat16 [320, 320], replicated
Inputs may be any that keep to these rules, and one draw needn't show every extreme that they name: `slot_start`: each image's 64 condition rows lie inside its own sequence of 512 tokens. `image_group`: every group denoises exactly one image.
All inputs are finite; a program needn't handle non-finite values.
Results may differ from a plain program's by a relative error of at most 0.035.
The roundings to bfloat16 on the way count: a program that leaves them out, or rounds other values in their place, can miss the bound.
Values may be sent and summed in bfloat16 or wider, within the bound.
A program may use at most 128 MiB of HBM per device.

v0:
```python
import math

import jax
import jax.numpy as jnp
from jax import lax
from jax.sharding import PartitionSpec as P

HEAD_DIM = 64
SLOTS = 64


def extended(cells, sides, width):
    for axis, dim in sides:
        count = lax.axis_size(axis)
        ends = count - 1
        head = lax.slice_in_dim(cells, 0, width, axis=dim)
        tail = lax.slice_in_dim(cells, cells.shape[dim] - width, cells.shape[dim], axis=dim)
        cells = jnp.concatenate(
            [
                lax.ppermute(tail, axis, [(i, (i + 1) % count) for i in range(ends)]),
                cells,
                lax.ppermute(head, axis, [((i + 1) % count, i) for i in range(ends)]),
            ],
            axis=dim,
        )
    return cells


def weighted_product(form, left, right):
    return jnp.einsum(form, left, right, preferred_element_type=jnp.float32)


def noise_levels():
    plan = jnp.linspace(0.00085**0.5, 0.012**0.5, 1000, dtype=jnp.float32) ** 2
    return jnp.exp(jnp.cumsum(jnp.log(1.0 - plan)))


def noisy_input(latent, noise_one, timestep):
    levels = noise_levels()
    picked = jnp.sum(jnp.where(jnp.arange(levels.shape[0]) == timestep, levels, 0.0))
    return (jnp.sqrt(picked) * latent + jnp.sqrt(1.0 - picked) * noise_one).astype(jnp.bfloat16)


def time_shift(timestep, channel_total):
    half_count = channel_total // 2
    frequency = jnp.exp(-math.log(10000.0) * jnp.arange(half_count, dtype=jnp.float32) / half_count)
    angles = timestep.astype(jnp.float32) * frequency
    return jnp.concatenate([jnp.cos(angles), jnp.sin(angles)])


def pad_columns(field):
    return jnp.pad(field, ((0, 0), (0, 0), (1, 1)))


def convolve(padded, weight, row_count, col_count):
    running = jnp.zeros((weight.shape[2], row_count * col_count), jnp.float32)
    for row_tap in range(3):
        for col_tap in range(3):
            window = padded[
                :, row_tap : row_tap + row_count, col_tap : col_tap + col_count
            ].reshape(padded.shape[0], row_count * col_count)
            running = running + jnp.dot(
                weight[row_tap, col_tap], window, preferred_element_type=jnp.float32
            )
    return running


def filter_grad(padded, upstream, row_count, col_count):
    tap_list = []
    for row_tap in range(3):
        for col_tap in range(3):
            window = padded[
                :, row_tap : row_tap + row_count, col_tap : col_tap + col_count
            ].reshape(padded.shape[0], row_count * col_count)
            tap_list.append(
                lax.dot_general(
                    upstream, window, (((1,), (1,)), ((), ())), preferred_element_type=jnp.float32
                )
            )
    return jnp.stack(tap_list).reshape(3, 3, upstream.shape[0], padded.shape[0])


def block_pass(
    noisy, timestep, group_kv, upstream, in_weight, res_weight, query_weight, out_weight
):
    channel_total = in_weight.shape[2]
    row_count, col_count = (noisy.shape[1], noisy.shape[2])
    latent_cell_count = row_count * col_count
    condition_slot_count = group_kv.shape[0]
    head_count = channel_total // HEAD_DIM
    logit_scale = HEAD_DIM ** (-0.5)
    noisy_pad = pad_columns(extended(noisy, (("row", 1),), 1))
    first = convolve(noisy_pad, in_weight, row_count, col_count)
    hidden_act = jax.nn.silu(first + time_shift(timestep, channel_total)[:, None]).astype(
        jnp.bfloat16
    )
    act_pad = pad_columns(
        extended(hidden_act.reshape(channel_total, row_count, col_count), (("row", 1),), 1)
    )
    residual = (first + convolve(act_pad, res_weight, row_count, col_count)).astype(jnp.bfloat16)
    query = jnp.dot(query_weight, residual, preferred_element_type=jnp.float32).astype(jnp.bfloat16)
    query_per_head = query.reshape(head_count, HEAD_DIM, latent_cell_count)
    key_matrix = group_kv[:, :channel_total].reshape(condition_slot_count, head_count, HEAD_DIM)
    value_matrix = group_kv[:, channel_total:].reshape(condition_slot_count, head_count, HEAD_DIM)
    score_matrix = weighted_product("isf,tis->itf", query_per_head, key_matrix) * logit_scale
    softmax_full = jax.nn.softmax(score_matrix, axis=1)
    softmax_reduced_precision = softmax_full.astype(jnp.bfloat16)
    attention_output = (
        weighted_product("cuo,ucb->cbo", softmax_reduced_precision, value_matrix)
        .astype(jnp.bfloat16)
        .reshape(channel_total, latent_cell_count)
    )
    block_out = (
        residual.astype(jnp.float32)
        + jnp.dot(out_weight, attention_output, preferred_element_type=jnp.float32)
    ).astype(jnp.bfloat16)
    upstream = upstream.reshape(channel_total, latent_cell_count)
    out_grad = lax.dot_general(
        upstream, attention_output, (((1,), (1,)), ((), ())), preferred_element_type=jnp.float32
    )
    grad_att = lax.dot_general(
        out_weight, upstream, (((0,), (0,)), ((), ())), preferred_element_type=jnp.float32
    ).astype(jnp.bfloat16)
    head_gradient = grad_att.reshape(head_count, HEAD_DIM, latent_cell_count)
    probability_gradient = weighted_product("isf,tis->itf", head_gradient, value_matrix)
    score_gradient = (
        logit_scale
        * softmax_full
        * (
            probability_gradient
            - jnp.sum(softmax_full * probability_gradient, axis=1, keepdims=True)
        )
    ).astype(jnp.bfloat16)
    query_gradient = (
        weighted_product("cuo,ucb->cbo", score_gradient, key_matrix)
        .astype(jnp.bfloat16)
        .reshape(channel_total, latent_cell_count)
    )
    key_gradient = weighted_product("exv,ewv->xew", score_gradient, query_per_head).reshape(
        condition_slot_count, channel_total
    )
    value_gradient = weighted_product(
        "exv,ewv->xew", softmax_reduced_precision, head_gradient
    ).reshape(condition_slot_count, channel_total)
    grad_kv = jnp.concatenate([key_gradient, value_gradient], axis=1)
    query_grad = lax.dot_general(
        query_gradient, residual, (((1,), (1,)), ((), ())), preferred_element_type=jnp.float32
    )
    grad_resid = (
        upstream.astype(jnp.float32)
        + lax.dot_general(
            query_weight,
            query_gradient,
            (((0,), (0,)), ((), ())),
            preferred_element_type=jnp.float32,
        )
    ).astype(jnp.bfloat16)
    res_grad = filter_grad(act_pad, grad_resid, row_count, col_count)
    return (
        block_out.reshape(channel_total, row_count, col_count),
        grad_kv,
        res_grad,
        query_grad,
        out_grad,
    )


def shards(
    llm_hidden,
    slot_start,
    image_group,
    timesteps,
    latents,
    noise,
    kv_weight,
    in_weight,
    res_weight,
    query_weight,
    out_weight,
    cotangent,
):
    own_index = lax.axis_index("img")
    condition = lax.dynamic_slice_in_dim(llm_hidden, slot_start[0], SLOTS, 0)
    kv_part = jnp.dot(condition, kv_weight, preferred_element_type=jnp.float32)
    source_group = lax.dynamic_index_in_dim(image_group, own_index, 0, keepdims=False)
    kv_whole = lax.psum(kv_part, "row").astype(jnp.bfloat16)
    selected = (image_group == own_index)[:, None, None]
    group_kv = jnp.sum(
        jnp.where(
            selected,
            lax.all_gather(kv_whole[None], "img", axis=0, tiled=True).astype(jnp.float32),
            0.0,
        ),
        axis=0,
    ).astype(jnp.bfloat16)
    noisy = noisy_input(latents[0], noise[0], timesteps[0])
    block_out, grad_kv, res_grad, query_grad, out_grad = block_pass(
        noisy, timesteps[0], group_kv, cotangent[0], in_weight, res_weight, query_weight, out_weight
    )
    grad_whole_kv = lax.psum(grad_kv.astype(jnp.bfloat16), "row")
    shard_piece = lax.all_gather(grad_whole_kv[None], "img", axis=0, tiled=True)
    indices = jnp.arange(shard_piece.shape[0], dtype=jnp.int32)
    selected = (indices == source_group)[:, None, None]
    grad_image = jnp.sum(jnp.where(selected, shard_piece.astype(jnp.float32), 0.0), axis=0).astype(
        jnp.bfloat16
    )
    grad_condition = lax.dot_general(
        grad_image, kv_weight, (((1,), (1,)), ((), ())), preferred_element_type=jnp.float32
    ).astype(jnp.bfloat16)
    grad_hidden = lax.dynamic_update_slice_in_dim(
        jnp.zeros_like(llm_hidden), grad_condition, slot_start[0], 0
    )
    kv_weight_part = lax.dot_general(
        condition, grad_image, (((0,), (0,)), ((), ())), preferred_element_type=jnp.float32
    )
    kv_weight_total = lax.psum(kv_weight_part.astype(jnp.bfloat16), "img").astype(jnp.float32)
    grad_kv_weight = (kv_weight_total * (lax.axis_size("img") * SLOTS) ** (-0.5)).astype(
        jnp.bfloat16
    )
    weight_scale = (
        lax.axis_size("img") * lax.axis_size("row") * latents.shape[2] * latents.shape[3]
    ) ** (-0.5)
    res_total, query_total, out_total = lax.psum((res_grad, query_grad, out_grad), ("img", "row"))
    grad_res_weight = (res_total * weight_scale).astype(jnp.bfloat16)
    grad_query_weight = (query_total * weight_scale).astype(jnp.bfloat16)
    grad_out_weight = (out_total * weight_scale).astype(jnp.bfloat16)
    return (
        block_out[None],
        grad_hidden,
        grad_kv_weight,
        grad_res_weight,
        grad_query_weight,
        grad_out_weight,
    )


def solution(mesh):
    return jax.shard_map(
        shards,
        mesh=mesh,
        in_specs=(
            P("img", "row"),
            P("img"),
            P(),
            P("img"),
            P("img", None, "row", None),
            P("img", None, "row", None),
            P("row", None),
            P(),
            P(),
            P(),
            P(),
            P("img", None, "row", None),
        ),
        out_specs=(P("img", None, "row", None), P("img", "row"), P("row", None), P(), P(), P()),
        check_vma=False,
    )
```

profile of v0, /device:TPU:1, one launch (start us, length us, event | category | flops | bytes accessed | tf_op | source)
XLA Modules:
  0.0 800.1 jit_solution(17061723320251089964)
XLA Ops:
  8.7 0.6 select_reduce_fusion.1
  10.7 0.7 add_convert_fusion
  11.5 4.0 collective-permute-start
  15.5 1.3 collective-permute-start.1
  17.5 1.5 fusion.87
  19.0 37.7 %all-reduce.14 = bf16[64,640]{1,0:T(8,128)(2,1)} all-reduce(f32[64,640]{1,0:T(8,128)S(1)} %fusion.87), channel_id=1, replica_groups=mesh['img'=32,'row'=8] {'row'}, use_global_device_ids=true, to_apply=%region_3.4 | all-reduce | flops 40960 | bytes 245760 | tf_op jit(solution)/shard_map/psum | solution.py:186
  56.9 1.4 convolution_convert_fusion.3
  62.5 1.3 collective-permute-start.2
  63.8 1.5 collective-permute-start.3
  65.3 0.7 collective-permute-done.2
  66.1 3.8 collective-permute-done.3
  69.9 0.6 pad_maximum_fusion
  70.6 2.7 fusion.7
  73.3 1.3 fusion.147
  80.5 49.0 %all-gather.6.cloned.1.call-done = bf16[2048,640]{1,0:T(8,128)(2,1)} async-done(((bf16[64,640]{1,0:T(8,128)(2,1)}), bf16[2048,640]{1,0:T(8,128)(2,1)}) %all-gather.6.cloned.1.call-update) | async-done | bytes 2621456 | tf_op jit(solution)/shard_map/all_gather | solution.py:191
  129.5 2.4 fusion.1
  132.1 0.8 copy.30
  132.9 1.7 fusion.151
  134.5 1.9 convolution_convert_fusion.6
  136.5 2.0 multiply_reduce_fusion
  138.9 0.7 copy-done.2
  140.1 0.7 maximum_bitcast_fusion
  140.9 77.7 %all-reduce.9.cloned.1.call-done = bf16[1,64,640]{2,1,0:T(8,128)(2,1)} async-done(((bf16[1,64,640]{2,1,0:T(8,128)(2,1)}), bf16[1,64,640]{2,1,0:T(8,128)(2,1)}) %all-reduce.9.cloned.1.call-update) | async-done | bytes 81936 | tf_op jit(solution)/shard_map/psum | solution.py:200
  219.2 1.0 copy-done.4
  220.5 0.8 copy-done.32
  221.3 1.3 convolution_bitcast_fusion.1
  222.6 1.3 fusion.152
  225.0 1.3 fusion.28
  226.3 1.3 fusion.27
  227.6 1.3 fusion.26
  228.9 1.3 fusion.25
  230.3 1.3 fusion.24
  231.6 1.3 fusion.23
  233.0 1.3 fusion.22
  234.3 1.3 fusion.21
  235.6 1.3 fusion.20
  237.6 0.6 iota_compare_fusion.5
  238.8 1.0 copy.59
  239.7 50.5 %all-gather.4.cloned.1.call-done = bf16[32,64,640]{2,1,0:T(8,128)(2,1)} async-done(((bf16[1,64,640]{2,1,0:T(8,128)(2,1)}), bf16[32,64,640]{2,1,0:T(8,128)(2,1)}) %all-gather.4.cloned.1.call-update) | async-done | bytes 2621456 | tf_op jit(solution)/shard_map/all_gather | solution.py:201
  290.2 2.4 select_reduce_fusion
  292.7 2.5 convolution_convert_fusion
  295.2 273.4 %all-reduce.13.cloned.1.call-done = (f32[3,3,320,320]{3,2,1,0:T(8,128)}, f32[320,320]{1,0:T(8,128)}, f32[320,320]{1,0:T(8,128)}) async-done(((f32[3,3,320,320]{3,2,1,0:T(8,128)}, f32[320,320]{1,0:T(8,128)}, f32[320,320]{1,0:T(8,128)}), (f32[3,3,320,320]{3,2,1,0:T(8,128)}, f32[320,320]{1,0:T(8,128)}, f32[320,320]{1,0:T(8,128)})) %all-reduce.13.cloned.1.call-update) | async-done | bytes 4505616 | tf_op jit(solution)/shard_map/psum | solution.py:223
  568.6 1.8 multiply_convert_fusion.4
  570.4 1.8 multiply_convert_fusion.3
  572.1 4.0 multiply_convert_fusion
  576.8 3.1 dynamic_update_slice.3
  579.9 211.2 %all-reduce.11.cloned.1.call-done = bf16[832,640]{1,0:T(8,128)(2,1)} async-done(((bf16[832,640]{1,0:T(8,128)(2,1)}), bf16[832,640]{1,0:T(8,128)(2,1)}) %all-reduce.11.cloned.1.call-update) | async-done | bytes 1064976 | tf_op jit(solution)/shard_map/psum | solution.py:216
  791.1 2.4 multiply_convert_fusion.1
  (127 shorter events, 15.7 us)
Async XLA Ops:
  7.2 10.3 %copy-start = (bf16[832,640]{1,0:T(8,128)(2,1)S(1)}, bf16[832,640]{1,0:T(8,128)(2,1)}, u32[]{:S(2)}) copy-start(bf16[832,640]{1,0:T(8,128)(2,1)} %param.18) | copy-start | bytes 3194884
  7.2 49.7 %copy-start.24 = (bf16[320,320]{1,0:T(8,128)(2,1)S(1)}, bf16[320,320]{1,0:T(8,128)(2,1)}, u32[]{:S(2)}) copy-start(bf16[320,320]{1,0:T(8,128)(2,1)} %param.22) | copy-start | bytes 614404
  7.2 49.7 %copy-start.31 = (bf16[1,320,8,128]{3,2,1,0:T(8,128)(2,1)S(1)}, bf16[1,320,8,128]{3,2,1,0:T(8,128)(2,1)}, u32[]{:S(2)}) copy-start(bf16[1,320,8,128]{3,2,1,0:T(8,128)(2,1)} %param.23) | copy-start | bytes 1966084
  7.2 122.3 %all-gather.6.cloned.1.call-start = ((), (), s32[]{:S(2)}) async-start(), calls=%async_computation.3 | async-start | bytes 2703360 | tf_op jit(solution)/shard_map/all_gather | solution.py:191
  11.5 46.9 %collective-permute-start = (bf16[4,1,128]{2,1,0:T(2,128)(2,1)S(1)}, bf16[4,1,128]{2,1,0:T(2,128)(2,1)S(1)}, u32[]{:S(2)}, u32[]{:S(2)}) collective-permute-start(bf16[4,1,128]{2,1,0:T(2,128)(2,1)S(1)} %get-tuple-element.29), channel_id=1, source_target_pairs={{0,1},{1,2},{2,3},{3,4},{4,5},{5,6},{6,7},{8,9},{9,10},{10,11},{11... | collective-permute-start | bytes 3080 | tf_op jit(solution)/shard_map/ppermute | solution.py:20
  15.5 42.8 %collective-permute-start.1 = (bf16[4,1,128]{2,1,0:T(2,128)(2,1)S(1)}, bf16[4,1,128]{2,1,0:T(2,128)(2,1)S(1)}, u32[]{:S(2)}, u32[]{:S(2)}) collective-permute-start(bf16[4,1,128]{2,1,0:T(2,128)(2,1)S(1)} %get-tuple-element.30), channel_id=1, source_target_pairs={{1,0},{2,1},{3,2},{4,3},{5,4},{6,5},{7,6},{9,8},{10,9},{11,10},{12... | collective-permute-start | bytes 3080 | tf_op jit(solution)/shard_map/ppermute | solution.py:22
  19.0 39.5 %copy-start.30 = (bf16[3,3,320,4]{2,3,1,0:T(4,128)(2,1)S(1)}, bf16[3,3,320,4]{2,3,1,0:T(4,128)(2,1)}, u32[]{:S(2)}) copy-start(bf16[3,3,320,4]{2,3,1,0:T(4,128)(2,1)} %param.19) | copy-start | bytes 69124
  56.7 161.9 %all-reduce.9.cloned.1.call-start = ((), (), s32[]{:S(2)}) async-start(), calls=%async_computation | async-start | bytes 163840 | tf_op jit(solution)/shard_map/psum | solution.py:200
  62.2 3.2 copy-start.33
  62.5 3.5 collective-permute-start.2
  63.8 6.1 collective-permute-start.3
  70.5 4.9 copy-start.7
  70.6 8.0 copy-start.5
  73.3 1.6 copy-start.21
  74.6 1.3 copy-start.17
  74.7 1.3 copy-start.15
  74.7 1.8 copy-start.13
  74.7 2.8 copy-start.11
  74.7 3.3 copy-start.9
  74.7 4.3 copy-start.19
  79.0 0.9 copy-start.23
  80.5 52.4 %copy-start.1 = (bf16[1024,320]{0,1:T(8,128)(2,1)}, bf16[1024,320]{0,1:T(8,128)(2,1)S(1)}, u32[]{:S(2)}) copy-start(bf16[1024,320]{0,1:T(8,128)(2,1)S(1)} %convolution_convert_fusion.1) | copy-start | bytes 1966084
  134.5 4.0 copy-start.26
  134.5 2.0 copy-start.28
  136.5 2.0 copy-start.3
  138.6 1.1 copy-start.2
  140.1 79.1 %copy-start.27 = (f32[5,1024]{1,0:T(8,128)S(1)}, f32[5,1024]{1,0:T(8,128)}, u32[]{:S(2)}) copy-start(f32[5,1024]{1,0:T(8,128)} %copy-done.26) | copy-start | bytes 61444
  140.8 78.4 %copy-start.29 = (bf16[64,320]{0,1:T(8,128)(2,1)S(1)}, bf16[64,320]{0,1:T(8,128)(2,1)}, u32[]{:S(2)}) copy-start(bf16[64,320]{0,1:T(8,128)(2,1)} %copy.30) | copy-start | bytes 122884
  140.9 149.4 %all-gather.4.cloned.1.call-start = ((), (), s32[]{:S(2)}) async-start(), calls=%async_computation.1 | async-start | bytes 2703360 | tf_op jit(solution)/shard_map/all_gather | solution.py:201
  218.6 350.0 %all-reduce.13.cloned.1.call-start = ((), (), s32[]{:S(2)}) async-start(), calls=%async_computation.4 | async-start | bytes 10813440 | tf_op jit(solution)/shard_map/psum | solution.py:223
  218.9 1.3 copy-start.4
  220.2 1.1 copy-start.32
  223.9 1.1 copy-start.18
  225.0 1.3 copy-start.8
  226.3 1.3 copy-start.16
  227.6 1.3 copy-start.14
  230.3 1.3 copy-start.12
  231.6 1.3 copy-start.10
  233.0 1.3 copy-start.6
  234.3 1.3 copy-start.20
  236.9 1.3 copy-start.25
  237.0 554.2 %all-reduce.11.cloned.1.call-start = ((), (), s32[]{:S(2)}) async-start(), calls=%async_computation.2 | async-start | bytes 2129920 | tf_op jit(solution)/shard_map/psum | solution.py:216
  579.9 213.6 %copy-start.22 = (bf16[512,832]{0,1:T(8,128)(2,1)}, bf16[512,832]{0,1:T(8,128)(2,1)S(1)}, u32[]{:S(2)}) copy-start(bf16[512,832]{0,1:T(8,128)(2,1)S(1)} %dynamic_update_slice.3) | copy-start | bytes 2555908
Sparse Core Ops, SparseCore 0:
  56.9 72.5 all-gather.5
  141.0 77.5 all-reduce.8
  220.6 69.5 all-gather.3
  297.5 271.0 all-reduce.12
  571.8 219.2 all-reduce.10
where the time goes:
time: 802 us; the launch traced here: 800 us
  waiting for transfers between devices  666 us (83%)
  blocking collectives  37.7 us (5%)
  matrix products  36.4 us (5%)
  other arithmetic  21.9 us (3%)
  between operations  17.3 us (2%)
  local copies, waits for them, and re-layouts  11.8 us (1%)
  starting transfers between devices  8.51 us (1%)
    psum x1, waiting for transfers between devices, shards(): lax.psum((res_grad, query_grad, out_grad), ('img', 'row'))  273 us
    psum x1, waiting for transfers between devices, shards(): lax.psum(kv_weight_part.astype(jnp.bfloat16), 'img').astype(jnp.float32)  211 us
    psum x1, waiting for transfers between devices, shards(): grad_whole_kv = lax.psum(grad_kv.astype(jnp.bfloat16), 'row')  77.7 us
    all_gather x1, waiting for transfers between devices, shards(): shard_piece = lax.all_gather(grad_whole_kv[None], 'img', axis=0, tiled=True)  50.5 us
    all_gather x1, waiting for transfers between devices, shards(): lax.all_gather(kv_whole[None], 'img', axis=0, tiled=True)  49 us
    psum x1, blocking collectives, shards(): kv_whole = lax.psum(kv_part, 'row').astype(jnp.bfloat16)  37.7 us
  transfers between devices with their start and end apart: 9, of which 7 were waited for; matrix products, arithmetic and copies ran while one was open for 6% of the time, Pallas kernels for 0%

commit v1 on v0

--- a/solution.py
+++ b/solution.py
@@ -1,12 +1,19 @@
+import functools
 import math
 
 import jax
 import jax.numpy as jnp
 from jax import lax
+from jax.experimental import pallas as pl
+from jax.experimental.pallas import tpu as pltpu
 from jax.sharding import PartitionSpec as P
 
 HEAD_DIM = 64
 SLOTS = 64
+MESH = pl.DeviceIdType.MESH
+CHANNELS = 320
+IMGS, ROWS = 32, 8
+F32, BF16 = jnp.float32, jnp.bfloat16
 
 
 def extended(cells, sides, width):
@@ -30,14 +37,9 @@
     return jnp.einsum(form, left, right, preferred_element_type=jnp.float32)
 
 
-def noise_levels():
+def noisy_input(latent, noise_one, timestep):
     plan = jnp.linspace(0.00085**0.5, 0.012**0.5, 1000, dtype=jnp.float32) ** 2
-    return jnp.exp(jnp.cumsum(jnp.log(1.0 - plan)))
-
-
-def noisy_input(latent, noise_one, timestep):
-    levels = noise_levels()
-    picked = jnp.sum(jnp.where(jnp.arange(levels.shape[0]) == timestep, levels, 0.0))
+    picked = jnp.exp(jnp.sum(jnp.where(jnp.arange(1000) <= timestep, jnp.log(1.0 - plan), 0.0)))
     return (jnp.sqrt(picked) * latent + jnp.sqrt(1.0 - picked) * noise_one).astype(jnp.bfloat16)
 
 
@@ -163,6 +165,545 @@
         query_grad,
         out_grad,
     )
+
+
+def place():
+    img, row = lax.axis_index("img"), lax.axis_index("row")
+    return img, row
+
+
+def coords(img, row):
+    z, low, core = lax.div(img, 4), lax.rem(lax.div(img, 2), 2), lax.rem(img, 2)
+    return z, lax.div(row, 4) * 2 + low, lax.rem(row, 4), core
+
+
+def device(z, x, y, core):
+    return (z * 4 + lax.rem(x, 2) * 2 + core, lax.div(x, 2) * 4 + y)
+
+
+def remote(src, dst, sems, slot, where):
+    return pltpu.make_async_remote_copy(
+        src_ref=src,
+        dst_ref=dst,
+        send_sem=sems.at[0, slot],
+        recv_sem=sems.at[1, slot],
+        device_id=where,
+        device_id_type=MESH,
+    )
+
+
+def each(count, act, first=1):
+    def body(k, carry):
+        act(k)
+        return carry
+
+    lax.fori_loop(first, count, body, 0)
+
+
+def rows16(index, count=16):
+    return pl.ds(pl.multiple_of(index * 16, 16), count)
+
+
+def greet(img, row, plane):
+    barrier = pltpu.get_barrier_semaphore()
+
+    def call(where):
+        pl.semaphore_signal(barrier, inc=1, device_id=where, device_id_type=MESH)
+
+    each(ROWS, lambda k: call((img, lax.rem(row + k, ROWS))))
+    each(IMGS, lambda k: call((lax.rem(img + k, IMGS), row)))
+    if plane:
+        z, x, y, core = coords(img, row)
+        other = 2 * (1 - lax.div(x, 2)) + (1 - lax.rem(x, 2))
+        call(device(z, other, y, core))
+    pl.semaphore_wait(barrier, ROWS - 1 + IMGS - 1 + int(plane))
+
+
+class RowSum:
+    def __init__(self, img, row, part, inbox, sems):
+        self.img, self.row, self.part, self.inbox, self.sems = img, row, part, inbox, sems
+
+    def copy(self, k):
+        r = lax.rem(self.row + k, ROWS)
+        src = self.part.at[lax.rem(r, 2), rows16(lax.div(r, 2))]
+        return remote(src, self.inbox.at[k - 1], self.sems, k - 1, (self.img, r))
+
+    def start(self):
+        each(ROWS, lambda k: self.copy(k).start())
+
+    def total(self):
+        own = self.part[lax.rem(self.row, 2), rows16(lax.div(self.row, 2))].astype(F32)
+
+        def body(k, acc):
+            self.copy(k).wait_recv()
+            return acc + self.inbox[k - 1].astype(F32)
+
+        return lax.fori_loop(1, ROWS, body, own)
+
+    def finish(self):
+        each(ROWS, lambda k: self.copy(k).wait_send())
+
+
+class Gather:
+    def __init__(self, count, me, where, target, sems):
+        self.count, self.me, self.where, self.target, self.sems = count, me, where, target, sems
+
+    def copy(self, k):
+        to = lax.rem(self.me + k, self.count)
+        return remote(
+            self.target(self.me), self.target(self.me), self.sems, k - 1, self.where(to)
+        )
+
+    def start(self):
+        each(self.count, lambda k: self.copy(k).start())
+
+    def wait(self):
+        each(self.count, lambda k: self.copy(k).wait_recv())
+
+    def finish(self):
+        each(self.count, lambda k: self.copy(k).wait_send())
+
+
+def front_kernel(
+    group_ref, slot_ref, hidden_ref, kvw_ref, cond_ref, kv_ref,
+    part, inbox, everyone, whole, sum_sems, img_sems, row_sems,
+):
+    img, row = place()
+    greet(img, row, False)
+    token = lax.broadcasted_iota(jnp.int32, (SLOTS, hidden_ref.shape[0]), 1)
+    wanted = lax.broadcasted_iota(jnp.int32, (SLOTS, hidden_ref.shape[0]), 0) + slot_ref[0]
+    pick = (token == wanted).astype(BF16)
+    cond_ref[...] = jnp.dot(pick, hidden_ref[...], preferred_element_type=F32).astype(BF16)
+    product = jnp.dot(cond_ref[...], kvw_ref[...], preferred_element_type=F32)
+    part[0] = product[:, :CHANNELS]
+    part[1] = product[:, CHANNELS:]
+    row_sum = RowSum(img, row, part, inbox, sum_sems)
+    row_sum.start()
+    everyone[img] = row_sum.total().astype(BF16)
+    gather = Gather(IMGS, img, lambda j: (j, row), lambda j: everyone.at[j], img_sems)
+    gather.start()
+    source = lax.fori_loop(
+        0, IMGS, lambda i, s: jnp.maximum(s, jnp.where(group_ref[i] == img, i, 0)), jnp.int32(0)
+    )
+    gather.wait()
+    whole[lax.rem(row, 2), rows16(lax.div(row, 2))] = everyone[source]
+    share = Gather(
+        ROWS, row, lambda j: (img, j),
+        lambda j: whole.at[lax.rem(j, 2), rows16(lax.div(j, 2))], row_sems,
+    )
+    share.start()
+    share.wait()
+    kv_ref[...] = whole[...]
+    row_sum.finish()
+    gather.finish()
+    share.finish()
+
+
+def front(llm_hidden, slot_start, image_group, kv_weight):
+    vmem, smem = pl.BlockSpec(memory_space=pltpu.VMEM), pl.BlockSpec(memory_space=pltpu.SMEM)
+    return pl.pallas_call(
+        front_kernel,
+        out_shape=(
+            jax.ShapeDtypeStruct((SLOTS, llm_hidden.shape[1]), BF16),
+            jax.ShapeDtypeStruct((2, SLOTS, CHANNELS), BF16),
+        ),
+        in_specs=[smem, smem, vmem, vmem],
+        out_specs=(vmem, vmem),
+        scratch_shapes=[
+            pltpu.VMEM((2, SLOTS, CHANNELS), F32),
+            pltpu.VMEM((ROWS - 1, 16, CHANNELS), F32),
+            pltpu.VMEM((IMGS, 16, CHANNELS), BF16),
+            pltpu.VMEM((2, SLOTS, CHANNELS), BF16),
+            pltpu.SemaphoreType.DMA((2, ROWS - 1)),
+            pltpu.SemaphoreType.DMA((2, IMGS - 1)),
+            pltpu.SemaphoreType.DMA((2, ROWS - 1)),
+        ],
+        compiler_params=pltpu.CompilerParams(
+            collective_id=0, has_side_effects=True, vmem_limit_bytes=32 * 2**20
+        ),
+        name="front",
+    )(image_group, slot_start, llm_hidden, kv_weight)
+
+
+A_ROWS, B_ROWS = 64, 48
+
+
+def total_of(count, base, piece):
+    return lax.fori_loop(1, count, lambda k, acc: acc + piece(k).astype(F32), base.astype(F32))
+
+
+def tail_kernel(
+    group_ref, slot_ref, grads_ref, gkv_ref, cond_ref, kvw_ref,
+    res_ref, query_ref, out_ref, hidden_ref, kvout_ref,
+    s_inbox, s_all, s_image,
+    in_core, half, in_a1, in_b1, sum_a, sum_b, in_a2, in_b2, sum_f, in_z, final,
+    k_part, k_core, k_half, k_low, k_quarter, k_z, k_final,
+    s_sum_sems, s_img_sems, s_row_sems,
+    core_sems, a1_sems, b1_sems, a2_sems, b2_sems, z_sems,
+    gz_sems, ga1_sems, gb1_sems, ga2_sems, gb2_sems, gcore_sems,
+    kc_sems, kx_sems, kz_sems, kgz_sems, kgx_sems, kgc_sems,
+    *, weight_scale, kv_scale,
+):
+    img, row = place()
+    z, x, y, core = coords(img, row)
+    partner = device(z, x, y, 1 - core)
+    low = lax.rem(x, 2)
+    across = device(z, x + 1 - 2 * low, y, core)
+    greet(img, row, True)
+
+    def at_x(k):
+        return lax.rem(x + k, 4)
+
+    def at_y(k):
+        return lax.rem(y + k, 4)
+
+    def at_z(k):
+        return lax.rem(z + k, 8)
+
+    row_sum = RowSum(img, row, gkv_ref, s_inbox, s_sum_sems)
+    row_sum.start()
+
+    def core_copy(k):
+        return remote(
+            grads_ref.at[1 - core, at_x(k)], in_core.at[at_x(k)], core_sems, k - 1, partner
+        )
+
+    each(5, lambda k: core_copy(k).start())
+
+    s_all[img] = row_sum.total().astype(BF16)
+    gather = Gather(IMGS, img, lambda j: (j, row), lambda j: s_all.at[j], s_img_sems)
+    gather.start()
+
+    def a1_copy(k):
+        return remote(
+            half.at[at_x(k), :, pl.ds(0, A_ROWS)], in_a1.at[k - 1], a1_sems, k - 1,
+            device(z, at_x(k), y, core),
+        )
+
+    def b1_copy(k):
+        return remote(
+            half.at[:, at_y(k), pl.ds(A_ROWS, B_ROWS)], in_b1.at[k - 1], b1_sems, k - 1,
+            device(z, x, at_y(k), core),
+        )
+
+    def add_core(k):
+        core_copy(k).wait_recv()
+        to = at_x(k)
+
+        def add(j):
+            half[to, j] = (
+                grads_ref[core, to, j].astype(F32) + in_core[to, j].astype(F32)
+            ).astype(BF16)
+
+        each(4, add, 0)
+
+    def add_and_send(k):
+        add_core(k)
+        a1_copy(k).start()
+
+    each(4, add_and_send)
+    add_core(4)
+    each(4, lambda k: b1_copy(k).start())
+
+    source = group_ref[img]
+    gather.wait()
+    s_image[lax.rem(row, 2), rows16(lax.div(row, 2))] = s_all[source]
+    share = Gather(
+        ROWS, row, lambda j: (img, j),
+        lambda j: s_image.at[lax.rem(j, 2), rows16(lax.div(j, 2))], s_row_sems,
+    )
+    share.start()
+
+    def a2_copy(k):
+        return remote(
+            sum_a.at[at_y(k)], in_a2.at[k - 1], a2_sems, k - 1, device(z, x, at_y(k), core)
+        )
+
+    def b2_copy(k):
+        return remote(
+            sum_b.at[at_x(k)], in_b2.at[k - 1], b2_sems, k - 1, device(z, at_x(k), y, core)
+        )
+
+    each(4, lambda k: a1_copy(k).wait_recv())
+
+    def add_a(j):
+        base = half[x, j, pl.ds(0, A_ROWS)]
+        sum_a[j] = total_of(4, base, lambda k: in_a1[k - 1, j]).astype(BF16)
+
+    each(4, add_a, 0)
+    each(4, lambda k: a2_copy(k).start())
+
+    share.wait()
+    feature_count = cond_ref.shape[1]
+    part = jnp.concatenate(
+        [
+            lax.dot_general(
+                cond_ref[...], s_image[side], (((0,), (0,)), ((), ())), preferred_element_type=F32
+            )
+            for side in range(2)
+        ],
+        axis=1,
+    ).astype(BF16)
+    k_part[pl.ds(0, feature_count)] = part
+    k_part[pl.ds(feature_count, 64)] = jnp.zeros((64, 2 * CHANNELS), BF16)
+
+    def kc_copy():
+        return remote(k_part.at[rows16((1 - core) * 28, 448)], k_core, kc_sems, 0, partner)
+
+    kc_copy().start()
+
+    each(4, lambda k: b1_copy(k).wait_recv())
+
+    def add_b(j):
+        base = half[j, y, pl.ds(A_ROWS, B_ROWS)]
+        sum_b[j] = total_of(4, base, lambda k: in_b1[k - 1, j]).astype(BF16)
+
+    each(4, add_b, 0)
+    each(4, lambda k: b2_copy(k).start())
+
+    each(4, lambda k: a2_copy(k).wait_recv())
+    sum_f[pl.ds(0, A_ROWS)] = total_of(4, sum_a[y], lambda k: in_a2[k - 1]).astype(BF16)
+    each(4, lambda k: b2_copy(k).wait_recv())
+    sum_f[pl.ds(A_ROWS, B_ROWS)] = total_of(4, sum_b[x], lambda k: in_b2[k - 1]).astype(BF16)
+
+    def z_copy(k):
+        to = at_z(k)
+        return remote(
+            sum_f.at[rows16(lax.rem(to, 7))], in_z.at[k - 1], z_sems, k - 1, device(to, x, y, core)
+        )
+
+    def to_owner(k, act):
+        pl.when(at_z(k) < 7)(lambda: act(k))
+
+    each(8, lambda k: to_owner(k, lambda j: z_copy(j).start()))
+
+    kc_copy().wait_recv()
+    each(
+        14,
+        lambda j: k_half.__setitem__(
+            rows16(2 * j, 32),
+            (
+                k_part[rows16(core * 28 + 2 * j, 32)].astype(F32) + k_core[rows16(2 * j, 32)].astype(F32)
+            ).astype(BF16),
+        ),
+        0,
+    )
+
+    def kx_copy():
+        return remote(k_half.at[rows16((1 - low) * 14, 224)], k_low, kx_sems, 0, across)
+
+    kx_copy().start()
+
+    @pl.when(z < 7)
+    def _():
+        each(8, lambda k: z_copy(k).wait_recv())
+        done = total_of(8, sum_f[rows16(z)], lambda k: in_z[k - 1]) * weight_scale
+        final[core, x, y, rows16(z)] = done.astype(BF16)
+
+    def gz_copy(k):
+        mine = final.at[core, x, y, rows16(lax.rem(z, 7))]
+        return remote(mine, mine, gz_sems, k - 1, device(at_z(k), x, y, core))
+
+    @pl.when(z < 7)
+    def _():
+        each(8, lambda k: gz_copy(k).start())
+
+    kx_copy().wait_recv()
+    each(
+        7,
+        lambda j: k_quarter.__setitem__(
+            rows16(2 * j, 32),
+            (
+                k_half[rows16(low * 14 + 2 * j, 32)].astype(F32) + k_low[rows16(2 * j, 32)].astype(F32)
+            ).astype(BF16),
+        ),
+        0,
+    )
+
+    def kz_copy(k):
+        to = at_z(k)
+        return remote(
+            k_quarter.at[rows16(2 * lax.rem(to, 7), 32)], k_z.at[k - 1], kz_sems, k - 1,
+            device(to, x, y, core),
+        )
+
+    each(8, lambda k: to_owner(k, lambda j: kz_copy(j).start()))
+
+    grad_condition = lax.dot_general(
+        jnp.concatenate([s_image[0], s_image[1]], axis=1), kvw_ref[...],
+        (((1,), (1,)), ((), ())), preferred_element_type=F32,
+    ).astype(BF16)
+    token = lax.broadcasted_iota(jnp.int32, (hidden_ref.shape[0], SLOTS), 0)
+    wanted = lax.broadcasted_iota(jnp.int32, (hidden_ref.shape[0], SLOTS), 1) + slot_ref[0]
+    put = (token == wanted).astype(BF16)
+    hidden_ref[...] = jnp.dot(put, grad_condition, preferred_element_type=F32).astype(BF16)
+
+    def from_owner(k, act):
+        pl.when(lax.rem(z + 8 - k, 8) < 7)(lambda: act(k))
+
+    each(8, lambda k: from_owner(k, lambda j: gz_copy(j).wait_recv()))
+
+    def ga1_copy(k):
+        mine = final.at[core, x, y, pl.ds(0, A_ROWS)]
+        return remote(mine, mine, ga1_sems, k - 1, device(z, x, at_y(k), core))
+
+    def gb1_copy(k):
+        mine = final.at[core, x, y, pl.ds(A_ROWS, B_ROWS)]
+        return remote(mine, mine, gb1_sems, k - 1, device(z, at_x(k), y, core))
+
+    each(4, lambda k: ga1_copy(k).start())
+    each(4, lambda k: gb1_copy(k).start())
+
+    @pl.when(z < 7)
+    def _():
+        each(8, lambda k: kz_copy(k).wait_recv())
+        done = total_of(8, k_quarter[rows16(2 * z, 32)], lambda k: k_z[k - 1]) * kv_scale
+        k_final[core, low, z] = done.astype(BF16)
+
+    def kgz_copy(k):
+        mine = k_final.at[core, low, lax.rem(z, 7)]
+        return remote(mine, mine, kgz_sems, k - 1, device(at_z(k), x, y, core))
+
+    @pl.when(z < 7)
+    def _():
+        each(8, lambda k: kgz_copy(k).start())
+
+    def ga2_copy(k):
+        mine = final.at[core, x, :, pl.ds(0, A_ROWS)]
+        return remote(mine, mine, ga2_sems, k - 1, device(z, at_x(k), y, core))
+
+    def gb2_copy(k):
+        mine = final.at[core, :, y, pl.ds(A_ROWS, B_ROWS)]
+        return remote(mine, mine, gb2_sems, k - 1, device(z, x, at_y(k), core))
+
+    def core_a(k):
+        mine = final.at[core, lax.rem(x + 4 - k, 4), :, pl.ds(0, A_ROWS)]
+        return remote(mine, mine, gcore_sems, k, partner)
+
+    def core_b(k):
+        mine = final.at[core, :, lax.rem(y + 4 - k, 4), pl.ds(A_ROWS, B_ROWS)]
+        return remote(mine, mine, gcore_sems, 4 + k, partner)
+
+    each(4, lambda k: ga1_copy(k).wait_recv())
+    each(4, lambda k: ga2_copy(k).start())
+    core_a(0).start()
+    each(4, lambda k: gb1_copy(k).wait_recv())
+    each(4, lambda k: gb2_copy(k).start())
+    core_b(0).start()
+
+    each(8, lambda k: from_owner(k, lambda j: kgz_copy(j).wait_recv()))
+
+    def kgx_copy():
+        mine = k_final.at[core, low]
+        return remote(mine, mine, kgx_sems, 0, across)
+
+    def kgc_copy(k):
+        mine = k_final.at[core, lax.rem(low + k, 2)]
+        return remote(mine, mine, kgc_sems, k, partner)
+
+    kgx_copy().start()
+    kgc_copy(0).start()
+
+    def pass_on_a(k):
+        ga2_copy(k).wait_recv()
+        core_a(k).start()
+
+    def pass_on_b(k):
+        gb2_copy(k).wait_recv()
+        core_b(k).start()
+
+    each(4, pass_on_a)
+    each(4, pass_on_b)
+    kgx_copy().wait_recv()
+    kgc_copy(1).start()
+
+    each(4, lambda k: core_a(k).wait_recv(), 0)
+    each(4, lambda k: core_b(k).wait_recv(), 0)
+
+    def write(target, begin, count):
+        for start in range(begin, begin + count, 16):
+            block, inside = divmod(start, 112)
+            c, rest = divmod(block, 16)
+            target[pl.ds(start - begin, 16)] = final[c, rest // 4, rest % 4, pl.ds(inside, 16)]
+
+    write(res_ref, 0, 2880)
+    write(query_ref, 2880, 320)
+    write(out_ref, 3200, 320)
+    each(2, lambda k: kgc_copy(k).wait_recv(), 0)
+    for block in range(26):
+        c, rest = divmod(block, 14)
+        kvout_ref[pl.ds(32 * block, 32)] = k_final[c, rest // 7, rest % 7]
+
+    row_sum.finish()
+    gather.finish()
+    share.finish()
+    each(5, lambda k: core_copy(k).wait_send())
+    for copy in (a1_copy, b1_copy, a2_copy, b2_copy, ga1_copy, gb1_copy, ga2_copy, gb2_copy):
+        each(4, lambda k, copy=copy: copy(k).wait_send())
+    each(8, lambda k: to_owner(k, lambda j: z_copy(j).wait_send()))
+    each(8, lambda k: to_owner(k, lambda j: kz_copy(j).wait_send()))
+
+    @pl.when(z < 7)
+    def _():
+        each(8, lambda k: gz_copy(k).wait_send())
+        each(8, lambda k: kgz_copy(k).wait_send())
+
+    each(4, lambda k: core_a(k).wait_send(), 0)
+    each(4, lambda k: core_b(k).wait_send(), 0)
+    kc_copy().wait_send()
+    kx_copy().wait_send()
+    kgx_copy().wait_send()
+    each(2, lambda k: kgc_copy(k).wait_send(), 0)
+
+
+def tail(image_group, slot_start, grads, grad_kv, condition, kv_weight, weight_scale, kv_scale):
+    vmem, smem = pl.BlockSpec(memory_space=pltpu.VMEM), pl.BlockSpec(memory_space=pltpu.SMEM)
+    width = CHANNELS
+    dma = lambda n: pltpu.SemaphoreType.DMA((2, n))
+    tokens = 512
+    return pl.pallas_call(
+        functools.partial(tail_kernel, weight_scale=weight_scale, kv_scale=kv_scale),
+        out_shape=(
+            jax.ShapeDtypeStruct((9 * width, width), BF16),
+            jax.ShapeDtypeStruct((width, width), BF16),
+            jax.ShapeDtypeStruct((width, width), BF16),
+            jax.ShapeDtypeStruct((tokens, condition.shape[1]), BF16),
+            jax.ShapeDtypeStruct(kv_weight.shape, BF16),
+        ),
+        in_specs=[smem, smem, vmem, vmem, vmem, vmem],
+        out_specs=(vmem,) * 5,
+        scratch_shapes=[
+            pltpu.VMEM((ROWS - 1, 16, width), BF16),
+            pltpu.VMEM((IMGS, 16, width), BF16),
+            pltpu.VMEM((2, SLOTS, width), BF16),
+            pltpu.VMEM((4, 4, 112, width), BF16),
+            pltpu.VMEM((4, 4, 112, width), BF16),
+            pltpu.VMEM((3, 4, A_ROWS, width), BF16),
+            pltpu.VMEM((3, 4, B_ROWS, width), BF16),
+            pltpu.VMEM((4, A_ROWS, width), BF16),
+            pltpu.VMEM((4, B_ROWS, width), BF16),
+            pltpu.VMEM((3, A_ROWS, width), BF16),
+            pltpu.VMEM((3, B_ROWS, width), BF16),
+            pltpu.VMEM((112, width), BF16),
+            pltpu.VMEM((7, 16, width), BF16),
+            pltpu.VMEM((2, 4, 4, 112, width), BF16),
+            pltpu.VMEM((896, 2 * width), BF16),
+            pltpu.VMEM((448, 2 * width), BF16),
+            pltpu.VMEM((448, 2 * width), BF16),
+            pltpu.VMEM((224, 2 * width), BF16),
+            pltpu.VMEM((224, 2 * width), BF16),
+            pltpu.VMEM((7, 32, 2 * width), BF16),
+            pltpu.VMEM((2, 2, 7, 32, 2 * width), BF16),
+            dma(7), dma(31), dma(7),
+            dma(4), dma(3), dma(3), dma(3), dma(3), dma(7),
+            dma(7), dma(3), dma(3), dma(3), dma(3), dma(8),
+            dma(1), dma(1), dma(7), dma(7), dma(1), dma(2),
+        ],
+        compiler_params=pltpu.CompilerParams(
+            collective_id=1, has_side_effects=True, vmem_limit_bytes=48 * 2**20
+        ),
+        name="tail",
+    )(image_group, slot_start, grads, grad_kv, condition, kv_weight)
 
 
 def shards(
@@ -179,59 +720,28 @@
     out_weight,
     cotangent,
 ):
-    own_index = lax.axis_index("img")
-    condition = lax.dynamic_slice_in_dim(llm_hidden, slot_start[0], SLOTS, 0)
-    kv_part = jnp.dot(condition, kv_weight, preferred_element_type=jnp.float32)
-    source_group = lax.dynamic_index_in_dim(image_group, own_index, 0, keepdims=False)
-    kv_whole = lax.psum(kv_part, "row").astype(jnp.bfloat16)
-    selected = (image_group == own_index)[:, None, None]
-    group_kv = jnp.sum(
-        jnp.where(
-            selected,
-            lax.all_gather(kv_whole[None], "img", axis=0, tiled=True).astype(jnp.float32),
-            0.0,
-        ),
-        axis=0,
-    ).astype(jnp.bfloat16)
+    condition, kv = front(llm_hidden, slot_start, image_group, kv_weight)
+    group_kv = jnp.concatenate([kv[0], kv[1]], axis=1)
     noisy = noisy_input(latents[0], noise[0], timesteps[0])
     block_out, grad_kv, res_grad, query_grad, out_grad = block_pass(
         noisy, timesteps[0], group_kv, cotangent[0], in_weight, res_weight, query_weight, out_weight
     )
-    grad_whole_kv = lax.psum(grad_kv.astype(jnp.bfloat16), "row")
-    shard_piece = lax.all_gather(grad_whole_kv[None], "img", axis=0, tiled=True)
-    indices = jnp.arange(shard_piece.shape[0], dtype=jnp.int32)
-    selected = (indices == source_group)[:, None, None]
-    grad_image = jnp.sum(jnp.where(selected, shard_piece.astype(jnp.float32), 0.0), axis=0).astype(
-        jnp.bfloat16
-    )
-    grad_condition = lax.dot_general(
-        grad_image, kv_weight, (((1,), (1,)), ((), ())), preferred_element_type=jnp.float32
-    ).astype(jnp.bfloat16)
-    grad_hidden = lax.dynamic_update_slice_in_dim(
-        jnp.zeros_like(llm_hidden), grad_condition, slot_start[0], 0
-    )
-    kv_weight_part = lax.dot_general(
-        condition, grad_image, (((0,), (0,)), ((), ())), preferred_element_type=jnp.float32
-    )
-    kv_weight_total = lax.psum(kv_weight_part.astype(jnp.bfloat16), "img").astype(jnp.float32)
-    grad_kv_weight = (kv_weight_total * (lax.axis_size("img") * SLOTS) ** (-0.5)).astype(
-        jnp.bfloat16
-    )
-    weight_scale = (
-        lax.axis_size("img") * lax.axis_size("row") * latents.shape[2] * latents.shape[3]
-    ) ** (-0.5)
-    res_total, query_total, out_total = lax.psum((res_grad, query_grad, out_grad), ("img", "row"))
-    grad_res_weight = (res_total * weight_scale).astype(jnp.bfloat16)
-    grad_query_weight = (query_total * weight_scale).astype(jnp.bfloat16)
-    grad_out_weight = (out_total * weight_scale).astype(jnp.bfloat16)
-    return (
-        block_out[None],
-        grad_hidden,
-        grad_kv_weight,
-        grad_res_weight,
-        grad_query_weight,
-        grad_out_weight,
-    )
+    grads = jnp.concatenate(
+        [
+            res_grad.reshape(-1, CHANNELS).astype(BF16),
+            query_grad.astype(BF16),
+            out_grad.astype(BF16),
+            jnp.zeros((64, CHANNELS), BF16),
+        ]
+    ).reshape(2, 4, 4, 112, CHANNELS)
+    grad_kv = grad_kv.astype(BF16)
+    grad_kv = jnp.stack([grad_kv[:, :CHANNELS], grad_kv[:, CHANNELS:]])
+    cells = IMGS * ROWS * latents.shape[2] * latents.shape[3]
+    res, query, out, grad_hidden, grad_kv_weight = tail(
+        image_group, slot_start, grads, grad_kv, condition, kv_weight,
+        cells ** (-0.5), (IMGS * SLOTS) ** (-0.5),
+    )
+    return (block_out[None], grad_hidden, grad_kv_weight, res.reshape(3, 3, CHANNELS, CHANNELS), query, out)
 
 
 def solution(mesh):

time: 802 us -> 197 us (0.25)
  waiting for transfers between devices: 666 us -> 4.41 us
  Pallas kernels: 0 us -> 113 us
  blocking collectives: 37.7 us -> 0 us
  between operations: 17.3 us -> 3.56 us
  local copies, waits for them, and re-layouts: 11.8 us -> 25 us
  other arithmetic: 21.9 us -> 12.1 us
    psum x3 -> x0, waiting for transfers between devices: 562 us -> none  [the longest x1 273 us: shards(): lax.psum((res_grad, query_grad, out_grad), ('img', 'row'))]
    pallas_call x0 -> x2, Pallas kernels: none -> 113 us  [the longest x1 77.5 us: tail(): pl.pallas_call(functools.partial(tail_kernel, weight_scale=weight_scale,...]
    all_gather x2 -> x0, waiting for transfers between devices: 99.5 us -> none  [the longest x1 50.5 us: shards(): shard_piece = lax.all_gather(grad_whole_kv[None], 'img', axis=0, tiled=True)]
    psum x1 -> x0, blocking collectives: 37.7 us -> none  [shards(): kv_whole = lax.psum(kv_part, 'row').astype(jnp.bfloat16)]
    unnamed x71 -> x99, local copies, waits for them, and re-layouts: 4.93 us -> 17.8 us
    convert_element_type x4 -> x0, other arithmetic: 9.94 us -> none  [the longest x1 4.02 us: shards(): grad_res_weight = (res_total * weight_scale).astype(jnp.bfloat16)]
  transfers between devices with their start and end apart: 9 -> 4, of which waited for: 7 -> 2; matrix products, arithmetic and copies ran while one was open for 6% -> 2% of each run, Pallas kernels for 0% -> 18%
where the time goes in v1:
time: 197 us; the launch traced here: 196 us
  Pallas kernels  113 us (57%)
  matrix products  29.5 us (15%)
  local copies, waits for them, and re-layouts  25 us (13%)
  other arithmetic  12.1 us (6%)
  starting transfers between devices  8.85 us (4%)
  waiting for transfers between devices  4.41 us (2%)
  between operations  3.56 us (2%)
    pallas_call x1, Pallas kernels, tail(): pl.pallas_call(functools.partial(tail_kernel, weight_scale=weight_scale,...  77.5 us
    pallas_call x1, Pallas kernels, front(): pl.pallas_call(front_kernel, out_shape=(jax.ShapeDtypeStruct((SLOTS, llm_...  35.2 us
    unnamed x99, local copies, waits for them, and re-layouts  17.8 us
    dot_general x18, matrix products, convolve(): jnp.dot(weight[row_tap, col_tap], window, preferred_element_type=jnp.floa...  9.08 us
    concatenate x1, other arithmetic, shards(): jnp.concatenate([res_grad.reshape(-1, CHANNELS).astype(BF16), query_grad....  6.57 us
    dot_general x9, matrix products, filter_grad(): lax.dot_general(upstream, window, (((1,), (1,)), ((), ())), preferred_ele...  6.27 us
    ppermute x2, starting transfers between devices, extended(): lax.ppermute(tail, axis, [(i, (i + 1) % count) for i in range(ends)])  6.26 us
    dot_general x5, matrix products, weighted_product(): return jnp.einsum(form, left, right, preferred_element_type=jnp.float32)  4.42 us
  transfers between devices with their start and end apart: 4, of which 2 were waited for; matrix products, arithmetic and copies ran while one was open for 2% of the time, Pallas kernels for 18%

profile of v1, /device:TPU:1, one launch (start us, length us, event | category | flops | bytes accessed | tf_op | source)
XLA Modules:
  0.0 196.1 jit_solution(68078309691157621)
XLA Ops:
  1.4 0.7 fusion.128
  2.9 0.7 add_convert_fusion
  3.6 4.0 %collective-permute-start = (bf16[4,1,128]{2,1,0:T(2,128)(2,1)S(1)}, bf16[4,1,128]{2,1,0:T(2,128)(2,1)S(1)}, u32[]{:S(2)}, u32[]{:S(2)}) collective-permute-start(bf16[4,1,128]{2,1,0:T(2,128)(2,1)S(1)} %get-tuple-element.52), channel_id=1, source_target_pairs={{0,1},{1,2},{2,3},{3,4},{4,5},{5,6},{6,7},{8,9},{9,10},{10,11},{11... | collective-permute-start | bytes 3080 | tf_op jit(solution)/shard_map/ppermute | solution.py:27
  7.7 1.3 collective-permute-start.1
  9.0 2.5 %convolution_convert_fusion.2 = bf16[320,1024]{1,0:T(8,128)(2,1)} fusion(bf16[320,320]{1,0:T(8,128)(2,1)S(1)} %copy-done, bf16[40,8,8,128]{3,2,1,0:T(8,128)(2,1)} %bitcast.314), kind=kOutput, calls=%fused_computation.38 | convolution fusion | flops 210042880 | bytes 1515520 | tf_op jit(solution)/shard_map/dot_general | solution.py:123
  12.3 0.6 copy.28.hidden_ref
  12.9 35.2 %front.1 = (bf16[64,832]{1,0:T(8,128)(2,1)S(1)}, bf16[2,64,320]{2,1,0:T(8,128)(2,1)S(1)}) custom-call(s32[32]{0:T(128)S(1)} %copy-done.11, s32[1]{0:T(128)S(6)} %copy.183.slot_ref, bf16[512,832]{1,0:T(8,128)(2,1)S(1)} %copy.28.hidden_ref, bf16[832,640]{1,0:T(8,128)(2,1)S(1)} %copy-done.1), custom_call_target="tpu_custom_call" | custom-call | tf_op jit(solution)/shard_map/front/pallas_call | solution.py:304
  51.4 1.6 fusion.17
  53.3 2.2 %collective-permute-start.2 = (bf16[320,1,128]{2,1,0:T(2,128)(2,1)S(1)}, bf16[320,1,128]{2,1,0:T(2,128)(2,1)S(1)}, u32[]{:S(2)}, u32[]{:S(2)}) collective-permute-start(bf16[320,1,128]{2,1,0:T(2,128)(2,1)S(1)} %get-tuple-element.40), channel_id=1, source_target_pairs={{0,1},{1,2},{2,3},{3,4},{4,5},{5,6},{6,7},{8,9},{9,10},{10,11},{11... | collective-permute-start | bytes 245768 | tf_op jit(solution)/shard_map/ppermute | solution.py:27
  55.6 1.3 collective-permute-start.3
  57.2 0.6 collective-permute-done.2
  57.8 3.8 %collective-permute-done.3 = bf16[320,1,128]{2,1,0:T(2,128)(2,1)S(1)} collective-permute-done((bf16[320,1,128]{2,1,0:T(2,128)(2,1)S(1)}, bf16[320,1,128]{2,1,0:T(2,128)(2,1)S(1)}, u32[]{:S(2)}, u32[]{:S(2)}) %collective-permute-start.3) | collective-permute-done | bytes 81952 | tf_op jit(solution)/shard_map/ppermute | solution.py:29
  61.7 0.7 copy-done.34
  62.3 2.9 %fusion.6 = bf16[320,10,130]{2,1,0:T(8,128)(2,1)S(1)} fusion(bf16[320,1,128]{2,1,0:T(2,128)(2,1)S(1)} %collective-permute-done.3, bf16[320,8,128]{2,1,0:T(8,128)(2,1)S(1)} %bitcast.278, bf16[320,1,128]{2,1,0:T(2,128)(2,1)S(1)} %collective-permute-done.2), kind=kLoop, calls=%fused_computation.9 | loop fusion | flops 4992000 | bytes 1651200 | tf_op jit(solution)/shard_map/concatenate | solution.py:25
  65.2 1.3 fusion.151
  66.6 0.8 copy-done.26
  67.9 0.6 pad_maximum_fusion
  72.5 0.8 copy-done.31
  74.8 1.7 fusion.155
  76.4 1.7 convolution_convert_fusion.3
  78.1 1.2 fusion.37
  79.4 1.3 fusion.18
  81.0 1.0 convolution_convert_fusion.15
  82.7 1.0 convolution_convert_fusion.16
  84.1 1.2 convolution_convert_fusion.5
  85.3 1.4 fusion.11
  86.7 0.7 copy.36
  87.4 1.0 copy.58
  88.4 1.1 copy.34
  89.5 1.9 copy.33
  91.4 1.6 copy.35
  93.0 1.7 fusion.20
  94.7 0.5 fusion.22
  95.8 0.5 fusion.24
  96.8 0.5 fusion.26
  97.4 0.5 fusion.28
  98.5 0.8 fusion.30
  102.8 6.6 %maximum_maximum_fusion = bf16[3584,320]{1,0:T(8,128)(2,1)} fusion(bf16[320,320]{1,0:T(8,128)(2,1)S(1)} %copy.34, bf16[320,320]{1,0:T(8,128)(2,1)S(1)} %copy-done.32, bf16[2880,320]{1,0:T(8,128)(2,1)S(1)} %bitcast.299, bf16[3584]{0:T(1024)(128)(2,1)S(1)} %pad.15.clone), kind=kLoop, calls=%fused_computation.7 | loop fusion | flops 9175040 | bytes 4553728 | tf_op jit(solution)/shard_map/concatenate | solution.py:729
  109.3 77.5 %tail.1 = (bf16[2880,320]{1,0:T(8,128)(2,1)S(1)}, bf16[320,320]{1,0:T(8,128)(2,1)S(1)}, bf16[320,320]{1,0:T(8,128)(2,1)S(1)}, bf16[512,832]{1,0:T(8,128)(2,1)S(1)}, bf16[832,640]{1,0:T(8,128)(2,1)S(1)}) custom-call(s32[32]{0:T(128)S(1)} %copy-done.11, s32[1]{0:T(128)S(6)} %copy.183.slot_ref, bf16[2,4,4,112,320]{4,3,2,1,0:T(8,128)(2,1)} %bitcast.276, ...), custom_call_target="tpu_custom_call" | custom-call | tf_op jit(solution)/shard_map/tail/pallas_call | solution.py:664
  186.8 1.0 copy-done.2
  187.8 0.9 copy-done.4
  188.7 0.7 copy-done.5
  189.4 0.7 copy-done.7
  190.1 2.3 %copy.37 = bf16[512,832]{0,1:T(8,128)(2,1)} copy(bf16[512,832]{1,0:T(8,128)(2,1)} %copy-done.4) | data formatting | bytes 1703936
  192.4 1.0 copy.185
  193.4 1.4 copy.186
  194.7 0.7 copy.187
  195.4 0.7 copy.188
  (124 shorter events, 16.3 us)
Async XLA Ops:
  0.6 8.4 %copy-start = (bf16[320,320]{1,0:T(8,128)(2,1)S(1)}, bf16[320,320]{1,0:T(8,128)(2,1)}, u32[]{:S(2)}) copy-start(bf16[320,320]{1,0:T(8,128)(2,1)} %param.22) | copy-start | bytes 614404
  0.6 11.6 %copy-start.33 = (bf16[512,832]{0,1:T(8,128)(2,1)S(1)}, bf16[512,832]{0,1:T(8,128)(2,1)}, u32[]{:S(2)}) copy-start(bf16[512,832]{0,1:T(8,128)(2,1)} %param.12) | copy-start | bytes 2555908
  3.6 44.5 %collective-permute-start = (bf16[4,1,128]{2,1,0:T(2,128)(2,1)S(1)}, bf16[4,1,128]{2,1,0:T(2,128)(2,1)S(1)}, u32[]{:S(2)}, u32[]{:S(2)}) collective-permute-start(bf16[4,1,128]{2,1,0:T(2,128)(2,1)S(1)} %get-tuple-element.52), channel_id=1, source_target_pairs={{0,1},{1,2},{2,3},{3,4},{4,5},{5,6},{6,7},{8,9},{9,10},{10,11},{11... | collective-permute-start | bytes 3080 | tf_op jit(solution)/shard_map/ppermute | solution.py:27
  7.7 40.5 %collective-permute-start.1 = (bf16[4,1,128]{2,1,0:T(2,128)(2,1)S(1)}, bf16[4,1,128]{2,1,0:T(2,128)(2,1)S(1)}, u32[]{:S(2)}, u32[]{:S(2)}) collective-permute-start(bf16[4,1,128]{2,1,0:T(2,128)(2,1)S(1)} %get-tuple-element.53), channel_id=1, source_target_pairs={{1,0},{2,1},{3,2},{4,3},{5,4},{6,5},{7,6},{9,8},{10,9},{11,10},{12... | collective-permute-start | bytes 3080 | tf_op jit(solution)/shard_map/ppermute | solution.py:29
  11.5 1.4 copy-start.1
  11.5 1.4 copy-start.11
  12.9 35.4 %copy-start.41 = (bf16[3,3,320,4]{2,3,1,0:T(4,128)(2,1)S(1)}, bf16[3,3,320,4]{2,3,1,0:T(4,128)(2,1)}, u32[]{:S(2)}) copy-start(bf16[3,3,320,4]{2,3,1,0:T(4,128)(2,1)} %param.19) | copy-start | bytes 69124
  48.1 1.0 copy-start.9
  53.3 4.5 %collective-permute-start.2 = (bf16[320,1,128]{2,1,0:T(2,128)(2,1)S(1)}, bf16[320,1,128]{2,1,0:T(2,128)(2,1)S(1)}, u32[]{:S(2)}, u32[]{:S(2)}) collective-permute-start(bf16[320,1,128]{2,1,0:T(2,128)(2,1)S(1)} %get-tuple-element.40), channel_id=1, source_target_pairs={{0,1},{1,2},{2,3},{3,4},{4,5},{5,6},{6,7},{8,9},{9,10},{10,11},{11... | collective-permute-start | bytes 245768 | tf_op jit(solution)/shard_map/ppermute | solution.py:27
  55.6 6.1 %collective-permute-start.3 = (bf16[320,1,128]{2,1,0:T(2,128)(2,1)S(1)}, bf16[320,1,128]{2,1,0:T(2,128)(2,1)S(1)}, u32[]{:S(2)}, u32[]{:S(2)}) collective-permute-start(bf16[320,1,128]{2,1,0:T(2,128)(2,1)S(1)} %get-tuple-element.41), channel_id=1, source_target_pairs={{1,0},{2,1},{3,2},{4,3},{5,4},{6,5},{7,6},{9,8},{10,9},{11,10},{12... | collective-permute-start | bytes 245768 | tf_op jit(solution)/shard_map/ppermute | solution.py:29
  65.2 2.2 %copy-start.30 = (bf16[3,3,320,320]{3,2,1,0:T(8,128)(2,1)S(1)}, bf16[3,3,320,320]{3,2,1,0:T(8,128)(2,1)}, u32[]{:S(2)}) copy-start(bf16[3,3,320,320]{3,2,1,0:T(8,128)(2,1)} %param.20) | copy-start | bytes 5529604
  66.6 0.8 copy-start.26
  66.6 2.8 %copy-start.24 = (bf16[320,8,128]{2,1,0:T(8,128)(2,1)}, bf16[320,8,128]{2,1,0:T(8,128)(2,1)S(1)}, u32[]{:S(2)}) copy-start(bf16[320,8,128]{2,1,0:T(8,128)(2,1)S(1)} %get-tuple-element.36) | copy-start | bytes 1966084
  66.6 3.3 %copy-start.22 = (bf16[320,8,128]{2,1,0:T(8,128)(2,1)}, bf16[320,8,128]{2,1,0:T(8,128)(2,1)S(1)}, u32[]{:S(2)}) copy-start(bf16[320,8,128]{2,1,0:T(8,128)(2,1)S(1)} %get-tuple-element.35) | copy-start | bytes 1966084
  66.6 4.4 %copy-start.20 = (bf16[320,8,128]{2,1,0:T(8,128)(2,1)}, bf16[320,8,128]{2,1,0:T(8,128)(2,1)S(1)}, u32[]{:S(2)}) copy-start(bf16[320,8,128]{2,1,0:T(8,128)(2,1)S(1)} %get-tuple-element.34) | copy-start | bytes 1966084
  66.6 4.9 %copy-start.18 = (bf16[320,8,128]{2,1,0:T(8,128)(2,1)}, bf16[320,8,128]{2,1,0:T(8,128)(2,1)S(1)}, u32[]{:S(2)}) copy-start(bf16[320,8,128]{2,1,0:T(8,128)(2,1)S(1)} %get-tuple-element.33) | copy-start | bytes 1966084
  66.6 5.9 %copy-start.28 = (bf16[320,8,128]{2,1,0:T(8,128)(2,1)}, bf16[320,8,128]{2,1,0:T(8,128)(2,1)S(1)}, u32[]{:S(2)}) copy-start(bf16[320,8,128]{2,1,0:T(8,128)(2,1)S(1)} %get-tuple-element.32) | copy-start | bytes 1966084
  66.6 1.3 copy-start.35
  68.6 0.8 copy-start.15
  68.6 3.4 %copy-start.13 = (bf16[320,8,128]{2,1,0:T(8,128)(2,1)}, bf16[320,8,128]{2,1,0:T(8,128)(2,1)S(1)}, u32[]{:S(2)}) copy-start(bf16[320,8,128]{2,1,0:T(8,128)(2,1)S(1)} %get-tuple-element.38) | copy-start | bytes 1966084
  72.0 1.3 copy-start.31
  73.3 0.9 copy-start.36
  76.4 1.7 copy-start.42
  79.4 1.4 copy-start.12
  79.4 1.6 copy-start.43
  83.7 1.5 copy-start.37
  85.3 1.4 copy-start.40
  85.3 2.1 %copy-start.17 = (bf16[40,8,8,128]{3,1,2,0:T(8,128)(2,1)S(1)}, bf16[40,8,8,128]{3,1,2,0:T(8,128)(2,1)}, u32[]{:S(2)}) copy-start(bf16[40,8,8,128]{3,1,2,0:T(8,128)(2,1)} %fusion.18) | copy-start | bytes 1966084
  86.7 6.3 %copy-start.27 = (bf16[320,8,128]{2,1,0:T(8,128)(2,1)S(1)}, bf16[320,8,128]{2,1,0:T(8,128)(2,1)}, u32[]{:S(2)}) copy-start(bf16[320,8,128]{2,1,0:T(8,128)(2,1)} %copy-done.26) | copy-start | bytes 1966084
  89.5 5.2 %copy-start.16 = (bf16[320,8,128]{2,1,0:T(8,128)(2,1)S(1)}, bf16[320,8,128]{2,1,0:T(8,128)(2,1)}, u32[]{:S(2)}) copy-start(bf16[320,8,128]{2,1,0:T(8,128)(2,1)} %copy-done.15) | copy-start | bytes 1966084
  93.0 1.7 copy-start.44
  94.7 1.1 copy-start.25
  95.8 1.1 copy-start.23
  97.4 1.1 copy-start.21
  98.5 1.1 copy-start.19
  99.6 1.1 copy-start.14
  100.7 1.1 copy-start.29
  101.8 0.8 copy-start.38
  101.8 0.8 copy-start.39
  101.8 1.0 copy-start.32
  102.8 6.6 %copy-start.10 = (bf16[64,832]{1,0:T(8,128)(2,1)S(1)}, bf16[64,832]{1,0:T(8,128)(2,1)}, u32[]{:S(2)}) copy-start(bf16[64,832]{1,0:T(8,128)(2,1)} %copy-done.9) | copy-start | bytes 319492
  186.8 1.0 copy-start.2
  187.8 0.9 copy-start.4
  188.7 0.7 copy-start.5
  189.4 0.7 copy-start.7
  190.1 2.3 %copy-start.3 = (bf16[832,640]{1,0:T(8,128)(2,1)S(1)}, bf16[832,640]{1,0:T(8,128)(2,1)}, u32[]{:S(2)}) copy-start(bf16[832,640]{1,0:T(8,128)(2,1)} %copy-done.2) | copy-start | bytes 3194884
  193.4 1.4 copy-start.8
  193.4 2.1 %copy-start.6 = (bf16[320,320]{1,0:T(8,128)(2,1)S(1)}, bf16[320,320]{1,0:T(8,128)(2,1)}, u32[]{:S(2)}) copy-start(bf16[320,320]{1,0:T(8,128)(2,1)} %copy-done.5) | copy-start | bytes 614404
  (1 other events, 0.7 us)

commit v2 on v1

v2 whole, which is shorter than its diff:
```python
import functools
import math

import jax
import jax.numpy as jnp
from jax import lax
from jax.experimental import pallas as pl
from jax.experimental.pallas import tpu as pltpu
from jax.sharding import PartitionSpec as P

HEAD_DIM = 64
SLOTS = 64
MESH = pl.DeviceIdType.MESH
CHANNELS = 320
HEADS = 5
IMGS, ROWS = 32, 8
TAPS = 11
F32, BF16 = jnp.float32, jnp.bfloat16


def place():
    img, row = lax.axis_index("img"), lax.axis_index("row")
    return img, row


def coords(img, row):
    z, low, core = lax.div(img, 4), lax.rem(lax.div(img, 2), 2), lax.rem(img, 2)
    return z, lax.div(row, 4) * 2 + low, lax.rem(row, 4), core


def device(z, x, y, core):
    return (z * 4 + lax.rem(x, 2) * 2 + core, lax.div(x, 2) * 4 + y)


def remote(src, dst, sems, slot, where):
    return pltpu.make_async_remote_copy(
        src_ref=src,
        dst_ref=dst,
        send_sem=sems.at[0, slot],
        recv_sem=sems.at[1, slot],
        device_id=where,
        device_id_type=MESH,
    )


def each(count, act, first=1):
    def body(k, carry):
        act(k)
        return carry

    lax.fori_loop(first, count, body, 0)


def rows16(index, count=16):
    return pl.ds(pl.multiple_of(index * 16, 16), count)


def greet(img, row):
    barrier = pltpu.get_barrier_semaphore()

    def call(where):
        pl.semaphore_signal(barrier, inc=1, device_id=where, device_id_type=MESH)

    each(ROWS, lambda k: call((img, lax.rem(row + k, ROWS))))
    each(IMGS, lambda k: call((lax.rem(img + k, IMGS), row)))
    z, x, y, core = coords(img, row)
    other = 2 * (1 - lax.div(x, 2)) + (1 - lax.rem(x, 2))
    call(device(z, other, y, core))
    return ROWS - 1 + IMGS - 1 + 1


class RowSum:
    def __init__(self, img, row, part, inbox, sems):
        self.img, self.row, self.part, self.inbox, self.sems = img, row, part, inbox, sems

    def copy(self, k):
        r = lax.rem(self.row + k, ROWS)
        src = self.part.at[lax.rem(r, 2), rows16(lax.div(r, 2))]
        return remote(src, self.inbox.at[k - 1], self.sems, k - 1, (self.img, r))

    def start(self):
        each(ROWS, lambda k: self.copy(k).start())

    def total(self):
        own = self.part[lax.rem(self.row, 2), rows16(lax.div(self.row, 2))].astype(F32)

        def body(k, acc):
            self.copy(k).wait_recv()
            return acc + self.inbox[k - 1].astype(F32)

        return lax.fori_loop(1, ROWS, body, own)

    def finish(self):
        each(ROWS, lambda k: self.copy(k).wait_send())


class Gather:
    def __init__(self, count, me, where, target, sems):
        self.count, self.me, self.where, self.target, self.sems = count, me, where, target, sems

    def copy(self, k):
        to = lax.rem(self.me + k, self.count)
        return remote(
            self.target(self.me), self.target(self.me), self.sems, k - 1, self.where(to)
        )

    def start(self):
        each(self.count, lambda k: self.copy(k).start())

    def wait(self):
        each(self.count, lambda k: self.copy(k).wait_recv())

    def finish(self):
        each(self.count, lambda k: self.copy(k).wait_send())


def total_of(count, base, piece):
    return lax.fori_loop(1, count, lambda k, acc: acc + piece(k).astype(F32), base.astype(F32))


def matmul(left, right):
    return jnp.dot(left, right, preferred_element_type=F32)


def against(left, right):
    return lax.dot_general(left, right, (((1,), (1,)), ((), ())), preferred_element_type=F32)


def shifted(field, step):
    lane = lax.broadcasted_iota(jnp.int32, (field.shape[0], 128), 1)
    edge = 127 if step > 0 else 0
    parts = []
    for start in range(0, field.shape[1], 128):
        turned = pltpu.roll(field[:, start : start + 128], (-step) % 128, 1)
        parts.append(jnp.where(lane == edge, 0.0, turned))
    return parts[0] if len(parts) == 1 else jnp.concatenate(parts, axis=1)


def spread(rows, target, flip):
    lane = lax.div(lax.broadcasted_iota(jnp.int32, rows.shape, 1), HEAD_DIM)
    wide = rows.astype(F32)
    full = jnp.concatenate([jnp.where(lane == h, wide, 0.0) for h in range(HEADS)], axis=0)
    target[...] = full.astype(BF16)
    flip[...] = full.T.astype(BF16)


def diagonal(full):
    lane = lax.div(lax.broadcasted_iota(jnp.int32, (SLOTS, CHANNELS), 1), HEAD_DIM)
    total = jnp.zeros((SLOTS, CHANNELS), F32)
    for h in range(HEADS):
        total = jnp.where(lane == h, full[h * SLOTS : (h + 1) * SLOTS], total)
    return total


def kernel(
    group_ref, slot_ref, time_ref,
    hidden_ref, kvw_ref, latent_ref, noise_ref, emb_ref, inw_ref, resw_ref, qw_ref, ow_ref, up_ref,
    block_ref, res_ref, query_ref, out_ref, ghidden_ref, kvout_ref,
    noisy, band, cond, part, f_inbox, f_all, f_kv, wcat, qw_t, ow_t, taps, first,
    hid, query, att, prob, gatt, gscore, gquery, ghid, bk, bk_t, bv, bv_t,
    gkv, s_inbox, s_all, s_image,
    grads, in_core, half, in_a1, in_b1, sum_a, sum_b, in_a2, in_b2, sum_f, in_z, final,
    k_part, k_core, k_half, k_low, k_quarter, k_z, k_final,
    halo_sems, f_sum_sems, f_img_sems, f_row_sems,
    s_sum_sems, s_img_sems, s_row_sems,
    core_sems, a1_sems, b1_sems, a2_sems, b2_sems, z_sems,
    gz_sems, ga1_sems, gb1_sems, ga2_sems, gb2_sems, gcore_sems,
    kc_sems, kx_sems, kz_sems, kgz_sems, kgx_sems, kgc_sems,
    *, weight_scale, kv_scale,
):
    img, row = place()
    z, x, y, core = coords(img, row)
    partner = device(z, x, y, 1 - core)
    low = lax.rem(x, 2)
    across = device(z, x + 1 - 2 * low, y, core)

    band[...] = jnp.zeros_like(band)
    signals = greet(img, row)

    def at_x(k):
        return lax.rem(x + k, 4)

    def at_y(k):
        return lax.rem(y + k, 4)

    def at_z(k):
        return lax.rem(z + k, 8)

    index = lax.broadcasted_iota(jnp.int32, (8, 128), 0) * 128 + lax.broadcasted_iota(
        jnp.int32, (8, 128), 1
    )
    share_of = index.astype(F32) / 999.0
    beta = (0.00085**0.5 * (1.0 - share_of) + 0.012**0.5 * share_of) ** 2
    logs = jnp.where(index <= time_ref[0], jnp.log(1.0 - jnp.where(index < 1000, beta, 0.0)), 0.0)
    level = jnp.exp(jnp.sum(logs, axis=(0, 1), keepdims=True))
    keep, add = jnp.sqrt(level), jnp.sqrt(1.0 - level)
    for c in range(4):
        noisy[c] = (keep * latent_ref[c] + add * noise_ref[c]).astype(BF16).astype(F32)
    for r in range(8):
        band[2 + r, pl.ds(0, 4)] = noisy[:, r, :]

    token = lax.broadcasted_iota(jnp.int32, (SLOTS, hidden_ref.shape[0]), 1)
    wanted = lax.broadcasted_iota(jnp.int32, (SLOTS, hidden_ref.shape[0]), 0) + slot_ref[0]
    cond[...] = matmul((token == wanted).astype(BF16), hidden_ref[...]).astype(BF16)
    product = matmul(cond[...], kvw_ref[...])
    part[0] = product[:, :CHANNELS]
    part[1] = product[:, CHANNELS:]

    pl.semaphore_wait(pltpu.get_barrier_semaphore(), signals)

    def halo_up():
        return remote(band.at[pl.ds(8, 2)], band.at[pl.ds(0, 2)], halo_sems, 0, (img, lax.rem(row + 1, ROWS)))

    def halo_down():
        return remote(band.at[pl.ds(2, 2)], band.at[pl.ds(10, 2)], halo_sems, 1, (img, lax.rem(row + ROWS - 1, ROWS)))

    above, below = row > 0, row < ROWS - 1
    pl.when(below)(lambda: halo_up().start())
    pl.when(above)(lambda: halo_down().start())
    f_sum = RowSum(img, row, part, f_inbox, f_sum_sems)
    f_sum.start()

    for a in range(3):
        for b in range(3):
            wcat[a, :, b * CHANNELS : (b + 1) * CHANNELS] = resw_ref[3 * a + b]
    qw_t[...] = qw_ref[...].astype(F32).T.astype(BF16)
    ow_t[...] = ow_ref[...].astype(F32).T.astype(BF16)

    pl.when(above)(lambda: halo_up().wait_recv())
    pl.when(below)(lambda: halo_down().wait_recv())

    def first_rows(j):
        fields = []
        for r in range(2):
            pieces = []
            for a in range(3):
                n = band[2 * j + r + a]
                pieces += [shifted(n, -1), n, shifted(n, 1)]
            fields.append(jnp.concatenate(pieces, axis=0))
        field = jnp.concatenate(fields, axis=1).astype(BF16)
        value = matmul(inw_ref[...], field)
        lanes = pl.ds(pl.multiple_of(j * 256, 256), 256)
        first[:, lanes] = value
        v = value + emb_ref[...]
        line = row * 8 - 1 + 2 * j + lax.div(lax.broadcasted_iota(jnp.int32, v.shape, 1), 128)
        act = jnp.where((line >= 0) & (line < 64), v / (1.0 + jnp.exp(-v)), 0.0)
        act = act.astype(BF16).astype(F32)
        taps[pl.ds(0, CHANNELS), lanes] = shifted(act, -1).astype(BF16)
        taps[pl.ds(CHANNELS, CHANNELS), lanes] = act.astype(BF16)
        taps[pl.ds(2 * CHANNELS, CHANNELS), lanes] = shifted(act, 1).astype(BF16)

    each(5, first_rows, 0)

    f_all[img] = f_sum.total().astype(BF16)
    f_gather = Gather(IMGS, img, lambda j: (j, row), lambda j: f_all.at[j], f_img_sems)
    f_gather.start()

    def cells(n, more=0):
        return pl.ds(pl.multiple_of(n * 256 + more, 128), 256)

    def residual(n):
        acc = first[:, cells(n, 128)]
        for a in range(3):
            acc = acc + matmul(wcat[a], taps[:, cells(n, 128 * a)])
        hid[:, cells(n)] = acc.astype(BF16)

    each(4, residual, 0)

    source = lax.fori_loop(
        0, IMGS, lambda i, s: jnp.maximum(s, jnp.where(group_ref[i] == img, i, 0)), jnp.int32(0)
    )
    f_gather.wait()
    f_kv[lax.rem(row, 2), rows16(lax.div(row, 2))] = f_all[source]
    f_share = Gather(
        ROWS, row, lambda j: (img, j),
        lambda j: f_kv.at[lax.rem(j, 2), rows16(lax.div(j, 2))], f_row_sems,
    )
    f_share.start()

    def projections(n):
        query[:, cells(n)] = matmul(qw_ref[...], hid[:, cells(n)]).astype(BF16)
        gatt[:, cells(n)] = matmul(ow_t[...], up_ref[:, cells(n)]).astype(BF16)

    each(4, projections, 0)
    f_share.wait()
    spread(f_kv[0], bk, bk_t)
    spread(f_kv[1], bv, bv_t)

    def attend(n):
        here = cells(n)
        score = matmul(bk[...], query[:, here]) * HEAD_DIM**-0.5
        score = score.reshape(HEADS, SLOTS, 256)
        top = jnp.max(score, axis=1, keepdims=True)
        grown = jnp.exp(score - top)
        soft = grown / jnp.sum(grown, axis=1, keepdims=True)
        soft_low = soft.reshape(CHANNELS, 256).astype(BF16)
        prob[:, here] = soft_low
        attended = matmul(bv_t[...], soft_low).astype(BF16)
        att[:, here] = attended
        block_ref[:, here] = (
            hid[:, here].astype(F32) + matmul(ow_ref[...], attended)
        ).astype(BF16)
        gprob = matmul(bv[...], gatt[:, here]).reshape(HEADS, SLOTS, 256)
        mean = jnp.sum(soft * gprob, axis=1, keepdims=True)
        gs = (HEAD_DIM**-0.5 * soft * (gprob - mean)).reshape(CHANNELS, 256).astype(BF16)
        gscore[:, here] = gs
        gq = matmul(bk_t[...], gs).astype(BF16)
        gquery[:, here] = gq
        ghid[:, here] = (up_ref[:, here].astype(F32) + matmul(qw_t[...], gq)).astype(BF16)

    each(4, attend, 0)

    gkv[0] = diagonal(against(gscore[...], query[...])).astype(BF16)
    gkv[1] = diagonal(against(prob[...], gatt[...])).astype(BF16)
    row_sum = RowSum(img, row, gkv, s_inbox, s_sum_sems)
    row_sum.start()

    def core_copy(t):
        return remote(
            grads.at[t, rows16((1 - core) * 10, 160)], in_core.at[t], core_sems, t, partner
        )

    grads[0] = against(gquery[...], hid[...]).astype(BF16)
    core_copy(0).start()
    grads[1] = against(up_ref[...], att[...]).astype(BF16)
    core_copy(1).start()

    def tap(t):
        a, b = lax.div(t - 2, 3), lax.rem(t - 2, 3)
        field = taps[
            pl.ds(pl.multiple_of(b * CHANNELS, CHANNELS), CHANNELS),
            pl.ds(pl.multiple_of(a * 128, 128), 1024),
        ]
        grads[t] = against(ghid[...], field).astype(BF16)
        core_copy(t).start()

    def a1_copy(k):
        return remote(
            half.at[at_x(k), :, pl.ds(0, 4)], in_a1.at[k - 1], a1_sems, k - 1,
            device(z, at_x(k), y, core),
        )

    def b1_copy(k):
        return remote(
            half.at[:, at_y(k), pl.ds(4, 3)], in_b1.at[k - 1], b1_sems, k - 1,
            device(z, x, at_y(k), core),
        )

    def add_block(to, begin, end):
        each(end, lambda t: core_copy(t).wait_recv(), begin)

        def add(u):
            unit = to * 28 + u
            t, j = lax.div(unit, 10), lax.rem(unit, 10)
            half[to, lax.div(u, 7), lax.rem(u, 7)] = (
                grads[t, rows16(core * 10 + j)].astype(F32) + in_core[t, rows16(j)].astype(F32)
            ).astype(BF16)

        each(26 if to == 3 else 28, add, 0)

        @pl.when(x != to)
        def _():
            a1_copy(lax.rem(to + 4 - x, 4)).start()

    half[3, 3, pl.ds(5, 2)] = jnp.zeros((2, 16, CHANNELS), BF16)
    each(5, tap, 2)
    add_block(0, 0, 3)
    s_all[img] = row_sum.total().astype(BF16)
    gather = Gather(IMGS, img, lambda j: (j, row), lambda j: s_all.at[j], s_img_sems)
    gather.start()
    each(8, tap, 5)
    add_block(1, 3, 6)
    each(11, tap, 8)
    add_block(2, 6, 9)
    add_block(3, 9, 11)
    each(4, lambda k: b1_copy(k).start())

    gather.wait()
    s_image[lax.rem(row, 2), rows16(lax.div(row, 2))] = s_all[group_ref[img]]
    share = Gather(
        ROWS, row, lambda j: (img, j),
        lambda j: s_image.at[lax.rem(j, 2), rows16(lax.div(j, 2))], s_row_sems,
    )
    share.start()

    def a2_copy(k):
        return remote(
            sum_a.at[at_y(k)], in_a2.at[k - 1], a2_sems, k - 1, device(z, x, at_y(k), core)
        )

    def b2_copy(k):
        return remote(
            sum_b.at[at_x(k)], in_b2.at[k - 1], b2_sems, k - 1, device(z, at_x(k), y, core)
        )

    each(4, lambda k: a1_copy(k).wait_recv())

    def add_a(j):
        sum_a[j] = total_of(4, half[x, j, pl.ds(0, 4)], lambda k: in_a1[k - 1, j]).astype(BF16)

    each(4, add_a, 0)
    each(4, lambda k: a2_copy(k).start())

    share.wait()
    features = cond.shape[1]
    for side in range(2):
        k_part[pl.ds(0, features), side * CHANNELS : (side + 1) * CHANNELS] = lax.dot_general(
            cond[...], s_image[side], (((0,), (0,)), ((), ())), preferred_element_type=F32
        ).astype(BF16)
    k_part[pl.ds(features, 64)] = jnp.zeros((64, 2 * CHANNELS), BF16)

    def kc_copy():
        return remote(k_part.at[rows16((1 - core) * 28, 448)], k_core, kc_sems, 0, partner)

    kc_copy().start()

    each(4, lambda k: b1_copy(k).wait_recv())

    def add_b(j):
        sum_b[j] = total_of(4, half[j, y, pl.ds(4, 3)], lambda k: in_b1[k - 1, j]).astype(BF16)

    each(4, add_b, 0)
    each(4, lambda k: b2_copy(k).start())

    each(4, lambda k: a2_copy(k).wait_recv())
    sum_f[pl.ds(0, 4)] = total_of(4, sum_a[y], lambda k: in_a2[k - 1]).astype(BF16)
    each(4, lambda k: b2_copy(k).wait_recv())
    sum_f[pl.ds(4, 3)] = total_of(4, sum_b[x], lambda k: in_b2[k - 1]).astype(BF16)

    def z_copy(k):
        to = at_z(k)
        return remote(
            sum_f.at[lax.rem(to, 7)], in_z.at[k - 1], z_sems, k - 1, device(to, x, y, core)
        )

    def to_owner(k, act):
        pl.when(at_z(k) < 7)(lambda: act(k))

    def from_owner(k, act):
        pl.when(lax.rem(z + 8 - k, 8) < 7)(lambda: act(k))

    each(8, lambda k: to_owner(k, lambda j: z_copy(j).start()))

    kc_copy().wait_recv()

    def add_kc(j):
        k_half[rows16(2 * j, 32)] = (
            k_part[rows16(core * 28 + 2 * j, 32)].astype(F32) + k_core[rows16(2 * j, 32)].astype(F32)
        ).astype(BF16)

    each(14, add_kc, 0)

    def kx_copy():
        return remote(k_half.at[rows16((1 - low) * 14, 224)], k_low, kx_sems, 0, across)

    kx_copy().start()

    @pl.when(z < 7)
    def _():
        each(8, lambda k: z_copy(k).wait_recv())
        done = total_of(8, sum_f[lax.rem(z, 7)], lambda k: in_z[k - 1]) * weight_scale
        final[core, x, y, lax.rem(z, 7)] = done.astype(BF16)

    def gz_copy(k):
        mine = final.at[core, x, y, lax.rem(z, 7)]
        return remote(mine, mine, gz_sems, k - 1, device(at_z(k), x, y, core))

    @pl.when(z < 7)
    def _():
        each(8, lambda k: gz_copy(k).start())

    kx_copy().wait_recv()

    def add_kx(j):
        k_quarter[rows16(2 * j, 32)] = (
            k_half[rows16(low * 14 + 2 * j, 32)].astype(F32) + k_low[rows16(2 * j, 32)].astype(F32)
        ).astype(BF16)

    each(7, add_kx, 0)

    def kz_copy(k):
        to = at_z(k)
        return remote(
            k_quarter.at[rows16(2 * lax.rem(to, 7), 32)], k_z.at[k - 1], kz_sems, k - 1,
            device(to, x, y, core),
        )

    each(8, lambda k: to_owner(k, lambda j: kz_copy(j).start()))

    gcond = against(jnp.concatenate([s_image[0], s_image[1]], axis=1), kvw_ref[...]).astype(BF16)
    spot = lax.broadcasted_iota(jnp.int32, (hidden_ref.shape[0], SLOTS), 0)
    slot = lax.broadcasted_iota(jnp.int32, (hidden_ref.shape[0], SLOTS), 1) + slot_ref[0]
    ghidden_ref[...] = matmul((spot == slot).astype(BF16), gcond).astype(BF16)

    each(8, lambda k: from_owner(k, lambda j: gz_copy(j).wait_recv()))

    def ga1_copy(k):
        mine = final.at[core, x, y, pl.ds(0, 4)]
        return remote(mine, mine, ga1_sems, k - 1, device(z, x, at_y(k), core))

    def gb1_copy(k):
        mine = final.at[core, x, y, pl.ds(4, 3)]
        return remote(mine, mine, gb1_sems, k - 1, device(z, at_x(k), y, core))

    each(4, lambda k: ga1_copy(k).start())
    each(4, lambda k: gb1_copy(k).start())

    @pl.when(z < 7)
    def _():
        each(8, lambda k: kz_copy(k).wait_recv())
        own = k_quarter[rows16(2 * lax.rem(z, 7), 32)]
        k_final[core, low, lax.rem(z, 7)] = (
            total_of(8, own, lambda k: k_z[k - 1]) * kv_scale
        ).astype(BF16)

    def kgz_copy(k):
        mine = k_final.at[core, low, lax.rem(z, 7)]
        return remote(mine, mine, kgz_sems, k - 1, device(at_z(k), x, y, core))

    @pl.when(z < 7)
    def _():
        each(8, lambda k: kgz_copy(k).start())

    def ga2_copy(k):
        mine = final.at[core, x, :, pl.ds(0, 4)]
        return remote(mine, mine, ga2_sems, k - 1, device(z, at_x(k), y, core))

    def gb2_copy(k):
        mine = final.at[core, :, y, pl.ds(4, 3)]
        return remote(mine, mine, gb2_sems, k - 1, device(z, x, at_y(k), core))

    def core_a(k):
        mine = final.at[core, lax.rem(x + 4 - k, 4), :, pl.ds(0, 4)]
        return remote(mine, mine, gcore_sems, k, partner)

    def core_b(k):
        mine = final.at[core, :, lax.rem(y + 4 - k, 4), pl.ds(4, 3)]
        return remote(mine, mine, gcore_sems, 4 + k, partner)

    each(4, lambda k: ga1_copy(k).wait_recv())
    each(4, lambda k: ga2_copy(k).start())
    core_a(0).start()
    each(4, lambda k: gb1_copy(k).wait_recv())
    each(4, lambda k: gb2_copy(k).start())
    core_b(0).start()

    each(8, lambda k: from_owner(k, lambda j: kgz_copy(j).wait_recv()))

    def kgx_copy():
        mine = k_final.at[core, low]
        return remote(mine, mine, kgx_sems, 0, across)

    def kgc_copy(k):
        mine = k_final.at[core, lax.rem(low + k, 2)]
        return remote(mine, mine, kgc_sems, k, partner)

    kgx_copy().start()
    kgc_copy(0).start()

    def pass_on_a(k):
        ga2_copy(k).wait_recv()
        core_a(k).start()

    def pass_on_b(k):
        gb2_copy(k).wait_recv()
        core_b(k).start()

    each(4, pass_on_a)
    each(4, pass_on_b)
    kgx_copy().wait_recv()
    kgc_copy(1).start()

    each(4, lambda k: core_a(k).wait_recv(), 0)
    each(4, lambda k: core_b(k).wait_recv(), 0)

    for t in range(TAPS):
        target, base = ((query_ref, 0), (out_ref, 0))[t] if t < 2 else (res_ref, (t - 2) * CHANNELS)
        for c in range(2):
            for j in range(10):
                block, inside = divmod(t * 10 + j, 7)
                target[pl.ds(base + c * 160 + j * 16, 16)] = final[c, block // 4, block % 4, inside]
    each(2, lambda k: kgc_copy(k).wait_recv(), 0)
    for block in range(26):
        c, rest = divmod(block, 14)
        kvout_ref[pl.ds(32 * block, 32)] = k_final[c, rest // 7, rest % 7]

    pl.when(below)(lambda: halo_up().wait_send())
    pl.when(above)(lambda: halo_down().wait_send())
    for one in (f_sum, f_gather, f_share, row_sum, gather, share):
        one.finish()
    each(TAPS, lambda t: core_copy(t).wait_send(), 0)
    for copy in (a1_copy, b1_copy, a2_copy, b2_copy, ga1_copy, gb1_copy, ga2_copy, gb2_copy):
        each(4, lambda k, copy=copy: copy(k).wait_send())
    each(8, lambda k: to_owner(k, lambda j: z_copy(j).wait_send()))
    each(8, lambda k: to_owner(k, lambda j: kz_copy(j).wait_send()))

    @pl.when(z < 7)
    def _():
        each(8, lambda k: gz_copy(k).wait_send())
        each(8, lambda k: kgz_copy(k).wait_send())

    each(4, lambda k: core_a(k).wait_send(), 0)
    each(4, lambda k: core_b(k).wait_send(), 0)
    kc_copy().wait_send()
    kx_copy().wait_send()
    kgx_copy().wait_send()
    each(2, lambda k: kgc_copy(k).wait_send(), 0)


def shards(
    llm_hidden,
    slot_start,
    image_group,
    timesteps,
    latents,
    noise,
    kv_weight,
    in_weight,
    res_weight,
    query_weight,
    out_weight,
    cotangent,
):
    width, features = CHANNELS, llm_hidden.shape[1]
    frequency = jnp.exp(-math.log(10000.0) * jnp.arange(width // 2, dtype=F32) / (width // 2))
    angles = timesteps[0].astype(F32) * frequency
    emb = jnp.concatenate([jnp.cos(angles), jnp.sin(angles)])[:, None]
    in_matrix = jnp.pad(in_weight.transpose(2, 0, 1, 3), ((0, 0), (0, 0), (0, 0), (0, 4)))
    vmem, smem = pl.BlockSpec(memory_space=pltpu.VMEM), pl.BlockSpec(memory_space=pltpu.SMEM)
    dma = lambda n: pltpu.SemaphoreType.DMA((2, n))
    low = lambda *shape: pltpu.VMEM(shape, BF16)
    field, square = low(width, 1024), low(width, width)
    out = lambda *shape: jax.ShapeDtypeStruct(shape, BF16)
    block, res, query, projection, grad_hidden, grad_kv_weight = pl.pallas_call(
        functools.partial(
            kernel,
            weight_scale=(IMGS * ROWS * 1024) ** (-0.5),
            kv_scale=(IMGS * SLOTS) ** (-0.5),
        ),
        out_shape=(
            out(width, 1024), out(9 * width, width), out(width, width), out(width, width),
            out(*llm_hidden.shape), out(*kv_weight.shape),
        ),
        in_specs=[smem] * 3 + [vmem] * 10,
        out_specs=(vmem,) * 6,
        scratch_shapes=[
            pltpu.VMEM((4, 8, 128), F32), pltpu.VMEM((12, 8, 128), F32),
            low(SLOTS, features), pltpu.VMEM((2, SLOTS, width), F32),
            pltpu.VMEM((ROWS - 1, 16, width), F32), low(IMGS, 16, width), low(2, SLOTS, width),
            low(3, width, 3 * width), square, square,
            low(3 * width, 1280), pltpu.VMEM((width, 1280), F32),
            field, field, field, field, field, field, field, field, square, square, square, square,
            low(2, SLOTS, width), low(ROWS - 1, 16, width), low(IMGS, 16, width), low(2, SLOTS, width),
            low(TAPS, width, width), low(TAPS, 160, width), low(4, 4, 7, 16, width),
            low(3, 4, 4, 16, width), low(3, 4, 3, 16, width),
            low(4, 4, 16, width), low(4, 3, 16, width), low(3, 4, 16, width), low(3, 3, 16, width),
            low(7, 16, width), low(7, 16, width), low(2, 4, 4, 7, 16, width),
            low(896, 2 * width), low(448, 2 * width), low(448, 2 * width), low(224, 2 * width),
            low(224, 2 * width), low(7, 32, 2 * width), low(2, 2, 7, 32, 2 * width),
            dma(2), dma(7), dma(31), dma(7), dma(7), dma(31), dma(7),
            dma(TAPS), dma(3), dma(3), dma(3), dma(3), dma(7),
            dma(7), dma(3), dma(3), dma(3), dma(3), dma(8),
            dma(1), dma(1), dma(7), dma(7), dma(1), dma(2),
        ],
        compiler_params=pltpu.CompilerParams(
            collective_id=0, has_side_effects=True, vmem_limit_bytes=60 * 2**20
        ),
        name="block",
    )(
        image_group, slot_start, timesteps, llm_hidden, kv_weight, latents[0], noise[0], emb,
        in_matrix.reshape(width, 72).astype(BF16), res_weight.reshape(9, width, width),
        query_weight, out_weight, cotangent.reshape(width, 1024),
    )
    return (
        block.reshape(1, width, 8, 128), grad_hidden, grad_kv_weight,
        res.reshape(3, 3, width, width), query, projection,
    )


def solution(mesh):
    return jax.shard_map(
        shards,
        mesh=mesh,
        in_specs=(
            P("img", "row"),
            P("img"),
            P(),
            P("img"),
            P("img", None, "row", None),
            P("img", None, "row", None),
            P("row", None),
            P(),
            P(),
            P(),
            P(),
            P("img", None, "row", None),
        ),
        out_specs=(P("img", None, "row", None), P("img", "row"), P("row", None), P(), P(), P()),
        check_vma=False,
    )
```

time: 197 us -> 125 us (0.63)
  matrix products: 29.5 us -> 0 us
  other arithmetic: 12.1 us -> 0.12 us
  local copies, waits for them, and re-layouts: 25 us -> 13.8 us
  starting transfers between devices: 8.85 us -> 0 us
  Pallas kernels: 113 us -> 108 us
  waiting for transfers between devices: 4.41 us -> 0 us
    dot_general x38 -> x0, matrix products: 27.9 us -> none  [the longest x18 9.08 us: convolve(): jnp.dot(weight[row_tap, col_tap], window, preferred_element_type=jnp.floa...]
    concatenate x5 -> x1, other arithmetic: 10.2 us -> 0.08 us  [shards(): emb = jnp.concatenate([jnp.cos(angles), jnp.sin(angles)])[:, None]]
    ppermute x4 -> x0, starting transfers between devices: 8.85 us -> none  [the longest x2 6.26 us: extended(): lax.ppermute(tail, axis, [(i, (i + 1) % count) for i in range(ends)])]
    unnamed x99 -> x18, local copies, waits for them, and re-layouts: 17.8 us -> 11.5 us
    pallas_call x2 -> x1, Pallas kernels: 113 us -> 108 us  [shards(): pl.pallas_call(functools.partial(kernel, weight_scale=(IMGS * ROWS * 1024...]
    ppermute x4 -> x0, waiting for transfers between devices: 4.41 us -> none  [the longest x2 3.83 us: extended(): lax.ppermute(head, axis, [((i + 1) % count, i) for i in range(ends)])]
    convert_element_type x2 -> x0, local copies, waits for them, and re-layouts: 2.98 us -> none  [the longest x1 1.86 us: shards(): query_grad.astype(BF16)]
    another operation x2 -> x0, local copies, waits for them, and re-layouts: 2.31 us -> none  [shards(): grad_kv = jnp.stack([grad_kv[:, :CHANNELS], grad_kv[:, CHANNELS:]])]
  transfers between devices with their start and end apart: 4 -> 0, of which waited for: 2 -> 0; matrix products, arithmetic and copies ran while one was open for 2% -> 0% of each run, Pallas kernels for 18% -> 0%
where the time goes in v2:
time: 125 us; the launch traced here: 124 us
  Pallas kernels  108 us (86%)
  local copies, waits for them, and re-layouts  13.8 us (11%)
  between operations  2.04 us (2%)
    pallas_call x1, Pallas kernels, shards(): pl.pallas_call(functools.partial(kernel, weight_scale=(IMGS * ROWS * 1024...  108 us
    unnamed x18, local copies, waits for them, and re-layouts  11.5 us

profile of v2, /device:TPU:1, one launch (start us, length us, event | category | flops | bytes accessed | tf_op | source)
XLA Modules:
  0.0 123.6 jit_solution(8303059944007008499)
XLA Ops:
  0.6 0.0 copy-start.2
  2.1 0.1 pad_maximum_fusion
  2.1 0.8 pad.4
  2.9 0.7 copy.23.inw_ref
  3.7 0.8 broadcast_in_dim.4.emb_ref
  4.4 2.0 %copy.28 = bf16[40,8,8,128]{3,1,2,0:T(8,128)(2,1)} copy(bf16[40,8,8,128]{3,2,1,0:T(8,128)(2,1)} %bitcast.18) | data formatting | bytes 1310720
  6.5 0.0 copy-done.2
  6.5 1.3 %copy.21.hidden_ref = bf16[512,832]{1,0:T(8,128)(2,1)} copy(bf16[512,832]{0,1:T(8,128)(2,1)S(1)} %copy-done.2) | data formatting | bytes 1703936 | tf_op args[0]
  7.7 107.6 %block.1 = (bf16[320,1024]{1,0:T(8,128)(2,1)}, bf16[2880,320]{1,0:T(8,128)(2,1)}, bf16[320,320]{1,0:T(8,128)(2,1)}, bf16[320,320]{1,0:T(8,128)(2,1)}, bf16[512,8...) custom-call(s32[32]{0:T(128)} %group_ref.1, s32[1]{0:T(128)S(6)} %copy.33.slot_ref, s32[1]{0:T(128)S(6)} %copy.34.time_ref, ...), custom_call_target="tpu_custom_call" | custom-call | tf_op jit(solution)/shard_map/block/pallas_call | solution.py:634
  115.4 0.0 copy-start.1
  115.4 2.1 %copy.26 = bf16[40,8,8,128]{3,2,1,0:T(8,128)(2,1)} copy(bf16[40,8,8,128]{3,1,2,0:T(8,128)(2,1)} %bitcast.20) | data formatting | bytes 1310720
  117.5 0.0 copy-start
  117.5 2.3 %copy.24 = bf16[512,832]{0,1:T(8,128)(2,1)} copy(bf16[512,832]{1,0:T(8,128)(2,1)} %get-tuple-element.25) | data formatting | bytes 1703936
  119.9 0.0 copy-done.1
  119.9 1.0 copy.35
  120.8 0.0 copy-done
  120.8 0.0 copy-start.4
  120.8 0.0 copy-start.3
  120.8 1.4 %copy.36 = bf16[3,3,320,320]{3,2,1,0:T(8,128)(2,1)} copy(bf16[3,3,320,320]{3,2,1,0:T(8,128)(2,1)S(1)} %bitcast.17) | data formatting | bytes 3686400
  122.2 0.0 copy-done.4
  122.2 0.7 copy.37
  122.9 0.0 copy-done.3
  122.9 0.7 copy.38
  (1 shorter events, 0.0 us)
Async XLA Ops:
  0.6 5.8 %copy-start.2 = (bf16[512,832]{0,1:T(8,128)(2,1)S(1)}, bf16[512,832]{0,1:T(8,128)(2,1)}, u32[]{:S(2)}) copy-start(bf16[512,832]{0,1:T(8,128)(2,1)} %param.12) | copy-start | bytes 2555908
  115.4 4.5 %copy-start.1 = (bf16[832,640]{1,0:T(8,128)(2,1)S(1)}, bf16[832,640]{1,0:T(8,128)(2,1)}, u32[]{:S(2)}) copy-start(bf16[832,640]{1,0:T(8,128)(2,1)} %get-tuple-element.40) | copy-start | bytes 3194884
  117.5 3.3 %copy-start = (bf16[2880,320]{1,0:T(8,128)(2,1)S(1)}, bf16[2880,320]{1,0:T(8,128)(2,1)}, u32[]{:S(2)}) copy-start(bf16[2880,320]{1,0:T(8,128)(2,1)} %get-tuple-element.15) | copy-start | bytes 5529604
  120.8 1.4 %copy-start.4 = (bf16[320,320]{1,0:T(8,128)(2,1)S(1)}, bf16[320,320]{1,0:T(8,128)(2,1)}, u32[]{:S(2)}) copy-start(bf16[320,320]{1,0:T(8,128)(2,1)} %get-tuple-element.42) | copy-start | bytes 614404
  120.8 2.1 %copy-start.3 = (bf16[320,320]{1,0:T(8,128)(2,1)S(1)}, bf16[320,320]{1,0:T(8,128)(2,1)}, u32[]{:S(2)}) copy-start(bf16[320,320]{1,0:T(8,128)(2,1)} %get-tuple-element.43) | copy-start | bytes 614404

commit v3 on v2

v3 whole, which is shorter than its diff:
```python
import functools
import math

import jax
import jax.numpy as jnp
from jax import lax
from jax.experimental import pallas as pl
from jax.experimental.pallas import tpu as pltpu
from jax.sharding import PartitionSpec as P

HEAD_DIM = 64
SLOTS = 64
MESH = pl.DeviceIdType.MESH
CHANNELS = 320
HEADS = 5
IMGS, ROWS = 32, 8
TAPS = 11
SLICES = 7
F32, BF16 = jnp.float32, jnp.bfloat16


def place():
    img, row = lax.axis_index("img"), lax.axis_index("row")
    return img, row


def coords(img, row):
    z, low, core = lax.div(img, 4), lax.rem(lax.div(img, 2), 2), lax.rem(img, 2)
    return z, lax.div(row, 4) * 2 + low, lax.rem(row, 4), core


def device(z, x, y, core):
    return (z * 4 + lax.rem(x, 2) * 2 + core, lax.div(x, 2) * 4 + y)


def remote(src, dst, sems, slot, where):
    return pltpu.make_async_remote_copy(
        src_ref=src,
        dst_ref=dst,
        send_sem=sems.at[0, slot],
        recv_sem=sems.at[1, slot],
        device_id=where,
        device_id_type=MESH,
    )


def each(count, act, first=1):
    def body(k, carry):
        act(k)
        return carry

    lax.fori_loop(first, count, body, 0)


def rows16(index, count=16):
    return pl.ds(pl.multiple_of(index * 16, 16), count)


def greet(img, row):
    barrier = pltpu.get_barrier_semaphore()

    def call(where):
        pl.semaphore_signal(barrier, inc=1, device_id=where, device_id_type=MESH)

    each(ROWS, lambda k: call((img, lax.rem(row + k, ROWS))))
    each(IMGS // 2, lambda k: call((lax.rem(img + 2 * k, IMGS), row)))
    call((img + 1 - 2 * lax.rem(img, 2), row))
    z, x, y, core = coords(img, row)
    other = 2 * (1 - lax.div(x, 2)) + (1 - lax.rem(x, 2))
    call(device(z, other, y, core))
    return ROWS - 1 + IMGS // 2 - 1 + 1 + 1


class RowSum:
    def __init__(self, img, row, part, inbox, sems):
        self.img, self.row, self.part, self.inbox, self.sems = img, row, part, inbox, sems

    def copy(self, k):
        r = lax.rem(self.row + k, ROWS)
        src = self.part.at[lax.rem(r, 2), rows16(lax.div(r, 2))]
        return remote(src, self.inbox.at[k - 1], self.sems, k - 1, (self.img, r))

    def start(self):
        each(ROWS, lambda k: self.copy(k).start())

    def total(self):
        own = self.part[lax.rem(self.row, 2), rows16(lax.div(self.row, 2))].astype(F32)

        def body(k, acc):
            self.copy(k).wait_recv()
            return acc + self.inbox[k - 1].astype(F32)

        return lax.fori_loop(1, ROWS, body, own)

    def finish(self):
        each(ROWS, lambda k: self.copy(k).wait_send())


class Gather:
    def __init__(self, count, me, where, target, sems):
        self.count, self.me, self.where, self.target, self.sems = count, me, where, target, sems

    def copy(self, k):
        to = lax.rem(self.me + k, self.count)
        return remote(
            self.target(self.me), self.target(self.me), self.sems, k - 1, self.where(to)
        )

    def start(self):
        each(self.count, lambda k: self.copy(k).start())

    def wait(self):
        each(self.count, lambda k: self.copy(k).wait_recv())

    def finish(self):
        each(self.count, lambda k: self.copy(k).wait_send())


class Pick:
    def __init__(self, img, row, everyone, give, got, sems, pair_sems):
        self.img, self.row, self.core = img, row, lax.rem(img, 2)
        self.everyone, self.give, self.got, self.pair_sems = everyone, give, got, pair_sems
        self.gather = Gather(
            IMGS // 2, lax.div(img, 2), lambda j: (2 * j + self.core, row),
            lambda j: everyone.at[j], sems,
        )

    def start(self, own):
        self.everyone[lax.div(self.img, 2)] = own
        self.gather.start()

    def pair(self):
        where = (self.img + 1 - 2 * self.core, self.row)
        return remote(self.give, self.got, self.pair_sems, 0, where)

    def relay(self, wanted):
        self.gather.wait()
        self.give[...] = self.everyone[lax.div(wanted, 2)]
        self.pair().start()

    def result(self, source):
        self.pair().wait_recv()
        own = self.everyone[lax.div(source, 2)].astype(F32)
        return jnp.where(lax.rem(source, 2) == self.core, own, self.got[...].astype(F32)).astype(BF16)

    def finish(self):
        self.gather.finish()
        self.pair().wait_send()


def total_of(count, base, piece):
    return lax.fori_loop(1, count, lambda k, acc: acc + piece(k).astype(F32), base.astype(F32))


def matmul(left, right):
    return jnp.dot(left, right, preferred_element_type=F32)


def against(left, right):
    return lax.dot_general(left, right, (((1,), (1,)), ((), ())), preferred_element_type=F32)


def shifted(field, step):
    lane = lax.broadcasted_iota(jnp.int32, (field.shape[0], 128), 1)
    edge = 127 if step > 0 else 0
    parts = []
    for start in range(0, field.shape[1], 128):
        turned = pltpu.roll(field[:, start : start + 128], (-step) % 128, 1)
        parts.append(jnp.where(lane == edge, 0.0, turned))
    return parts[0] if len(parts) == 1 else jnp.concatenate(parts, axis=1)


def spread(rows, target, flip):
    lane = lax.div(lax.broadcasted_iota(jnp.int32, rows.shape, 1), HEAD_DIM)
    wide = rows.astype(F32)
    full = jnp.concatenate([jnp.where(lane == h, wide, 0.0) for h in range(HEADS)], axis=0)
    target[...] = full.astype(BF16)
    flip[...] = full.T.astype(BF16)


def diagonal(full):
    lane = lax.div(lax.broadcasted_iota(jnp.int32, (SLOTS, CHANNELS), 1), HEAD_DIM)
    total = jnp.zeros((SLOTS, CHANNELS), F32)
    for h in range(HEADS):
        total = jnp.where(lane == h, full[h * SLOTS : (h + 1) * SLOTS], total)
    return total


def kernel(
    group_ref, slot_ref, time_ref,
    hidden_ref, kvw_ref, latent_ref, noise_ref, emb_ref, inw_ref, qw_ref, ow_ref, resw_hbm, up_hbm,
    block3_ref, res_ref, query_ref, out_ref, ghidden_ref, kvout_ref,
    resw_ref, up3_ref, load_sems, turn, up_ref, block_ref,
    noisy, band, cond, part, f_inbox, f_all, f_give, f_got, f_kv, wcat, qw_t, ow_t, taps, first,
    hid, query, att, prob, gatt, gscore, gquery, ghid, bk, bk_t, bv, bv_t,
    gkv, s_inbox, s_all, s_give, s_got, s_image,
    grads, in_core, half, in_1, mid, in_2, sum_f, in_z, final,
    k_part, k_core, k_half, k_low1, k_z1, k_sum1, k_sum2, k_z2, k_low2, k_final,
    halo_sems, f_sum_sems, f_img_sems, f_pair_sems, f_row_sems,
    s_sum_sems, s_img_sems, s_pair_sems, s_row_sems,
    core_sems, s1_sems, s2_sems, z_sems,
    gz_sems, g1_sems, g2_sems, gcore_sems,
    kc_sems, kx1_sems, kz1_sems, kx2_sems, kz2_sems,
    kgx1_sems, kgz1_sems, kgx2_sems, kgz2_sems, kgc_sems,
    *, weight_scale, kv_scale,
):
    loads = [
        pltpu.make_async_copy(resw_hbm, resw_ref, load_sems.at[0]),
        pltpu.make_async_copy(up_hbm, up3_ref, load_sems.at[1]),
    ]
    for load in loads:
        load.start()
    img, row = place()
    z, x, y, core = coords(img, row)
    partner = device(z, x, y, 1 - core)
    low = lax.rem(x, 2)
    across = device(z, x + 1 - 2 * low, y, core)

    band[...] = jnp.zeros_like(band)
    signals = greet(img, row)

    def at_x(k):
        return lax.rem(x + k, 4)

    def at_y(k):
        return lax.rem(y + k, 4)

    def at_z(k):
        return lax.rem(z + k, 8)

    token = lax.broadcasted_iota(jnp.int32, (SLOTS, hidden_ref.shape[0]), 1)
    wanted = lax.broadcasted_iota(jnp.int32, (SLOTS, hidden_ref.shape[0]), 0) + slot_ref[0]
    cond[...] = matmul((token == wanted).astype(BF16), hidden_ref[...]).astype(BF16)
    product = matmul(cond[...], kvw_ref[...])
    part[0] = product[:, :CHANNELS]
    part[1] = product[:, CHANNELS:]

    index = lax.broadcasted_iota(jnp.int32, (8, 128), 0) * 128 + lax.broadcasted_iota(
        jnp.int32, (8, 128), 1
    )
    share_of = index.astype(F32) / 999.0
    beta = (0.00085**0.5 * (1.0 - share_of) + 0.012**0.5 * share_of) ** 2
    logs = jnp.where(index <= time_ref[0], jnp.log(1.0 - jnp.where(index < 1000, beta, 0.0)), 0.0)
    level = jnp.exp(jnp.sum(logs, axis=(0, 1), keepdims=True))
    keep, add = jnp.sqrt(level), jnp.sqrt(1.0 - level)
    for c in range(4):
        noisy[c] = (keep * latent_ref[c] + add * noise_ref[c]).astype(BF16).astype(F32)
    for r in range(8):
        band[2 + r, pl.ds(0, 4)] = noisy[:, r, :]

    pl.semaphore_wait(pltpu.get_barrier_semaphore(), signals)

    def halo_up():
        return remote(band.at[pl.ds(8, 2)], band.at[pl.ds(0, 2)], halo_sems, 0, (img, lax.rem(row + 1, ROWS)))

    def halo_down():
        return remote(band.at[pl.ds(2, 2)], band.at[pl.ds(10, 2)], halo_sems, 1, (img, lax.rem(row + ROWS - 1, ROWS)))

    above, below = row > 0, row < ROWS - 1
    pl.when(below)(lambda: halo_up().start())
    pl.when(above)(lambda: halo_down().start())
    f_sum = RowSum(img, row, part, f_inbox, f_sum_sems)
    f_sum.start()

    loads[0].wait()
    for a in range(3):
        for b in range(3):
            wcat[a, :, b * CHANNELS : (b + 1) * CHANNELS] = resw_ref[3 * a + b]
    qw_t[...] = qw_ref[...].astype(F32).T.astype(BF16)
    ow_t[...] = ow_ref[...].astype(F32).T.astype(BF16)

    def source_of(which):
        return lax.fori_loop(
            0, IMGS, lambda i, s: jnp.maximum(s, jnp.where(group_ref[i] == which, i, 0)), jnp.int32(0)
        )

    other = img + 1 - 2 * core
    source, other_source = source_of(img), source_of(other)
    f_pick = Pick(img, row, f_all, f_give, f_got, f_img_sems, f_pair_sems)
    f_pick.start(f_sum.total().astype(BF16))

    pl.when(above)(lambda: halo_up().wait_recv())
    pl.when(below)(lambda: halo_down().wait_recv())

    def first_rows(j):
        fields = []
        for r in range(2):
            pieces = []
            for a in range(3):
                n = band[2 * j + r + a]
                pieces += [shifted(n, -1), n, shifted(n, 1)]
            fields.append(jnp.concatenate(pieces, axis=0))
        field = jnp.concatenate(fields, axis=1).astype(BF16)
        value = matmul(inw_ref[...], field)
        lanes = pl.ds(pl.multiple_of(j * 256, 256), 256)
        first[:, lanes] = value
        v = value + emb_ref[...]
        line = row * 8 - 1 + 2 * j + lax.div(lax.broadcasted_iota(jnp.int32, v.shape, 1), 128)
        act = jnp.where((line >= 0) & (line < 64), v / (1.0 + jnp.exp(-v)), 0.0)
        act = act.astype(BF16).astype(F32)
        taps[pl.ds(0, CHANNELS), lanes] = shifted(act, -1).astype(BF16)
        taps[pl.ds(CHANNELS, CHANNELS), lanes] = act.astype(BF16)
        taps[pl.ds(2 * CHANNELS, CHANNELS), lanes] = shifted(act, 1).astype(BF16)

    each(5, first_rows, 0)

    def cells(n, more=0):
        return pl.ds(pl.multiple_of(n * 256 + more, 128), 256)

    def residual(n):
        acc = first[:, cells(n, 128)]
        for a in range(3):
            acc = acc + matmul(wcat[a], taps[:, cells(n, 128 * a)])
        hid[:, cells(n)] = acc.astype(BF16)

    each(2, residual, 0)
    f_pick.relay(other_source)
    each(4, residual, 2)

    f_kv[lax.rem(row, 2), rows16(lax.div(row, 2))] = f_pick.result(source)
    f_share = Gather(
        ROWS, row, lambda j: (img, j),
        lambda j: f_kv.at[lax.rem(j, 2), rows16(lax.div(j, 2))], f_row_sems,
    )
    f_share.start()

    loads[1].wait()

    def flatten(c):
        channels = rows16(4 * c, 64)
        turn[...] = up3_ref[channels].astype(F32)
        for r in range(8):
            up_ref[channels, r * 128 : (r + 1) * 128] = turn[:, r, :].astype(BF16)

    each(5, flatten, 0)

    def unflatten(c):
        channels = rows16(4 * c, 64)
        for r in range(8):
            turn[:, r, :] = block_ref[channels, r * 128 : (r + 1) * 128].astype(F32)
        block3_ref[channels] = turn[...].astype(BF16)

    def projections(n):
        query[:, cells(n)] = matmul(qw_ref[...], hid[:, cells(n)]).astype(BF16)
        gatt[:, cells(n)] = matmul(ow_t[...], up_ref[:, cells(n)]).astype(BF16)

    each(4, projections, 0)
    f_share.wait()
    spread(f_kv[0], bk, bk_t)
    spread(f_kv[1], bv, bv_t)

    def attend(n):
        here = cells(n)
        score = matmul(bk[...], query[:, here]) * HEAD_DIM**-0.5
        score = score.reshape(HEADS, SLOTS, 256)
        top = jnp.max(score, axis=1, keepdims=True)
        grown = jnp.exp(score - top)
        soft = grown / jnp.sum(grown, axis=1, keepdims=True)
        soft_low = soft.reshape(CHANNELS, 256).astype(BF16)
        prob[:, here] = soft_low
        gprob = matmul(bv[...], gatt[:, here]).reshape(HEADS, SLOTS, 256)
        mean = jnp.sum(soft * gprob, axis=1, keepdims=True)
        gs = (HEAD_DIM**-0.5 * soft * (gprob - mean)).reshape(CHANNELS, 256).astype(BF16)
        gscore[:, here] = gs

    def attend_more(n):
        here = cells(n)
        attended = matmul(bv_t[...], prob[:, here]).astype(BF16)
        att[:, here] = attended
        block_ref[:, here] = (
            hid[:, here].astype(F32) + matmul(ow_ref[...], attended)
        ).astype(BF16)
        gq = matmul(bk_t[...], gscore[:, here]).astype(BF16)
        gquery[:, here] = gq
        ghid[:, here] = (up_ref[:, here].astype(F32) + matmul(qw_t[...], gq)).astype(BF16)

    each(4, attend, 0)

    gkv[0] = diagonal(against(gscore[...], query[...])).astype(BF16)
    gkv[1] = diagonal(against(prob[...], gatt[...])).astype(BF16)
    row_sum = RowSum(img, row, gkv, s_inbox, s_sum_sems)
    row_sum.start()

    each(4, attend_more, 0)

    def core_copy(t):
        return remote(
            grads.at[t, rows16((1 - core) * 10, 160)], in_core.at[t], core_sems, t, partner
        )

    grads[0] = against(gquery[...], hid[...]).astype(BF16)
    core_copy(0).start()
    grads[1] = against(up_ref[...], att[...]).astype(BF16)
    core_copy(1).start()

    def tap(t):
        a, b = lax.div(t - 2, 3), lax.rem(t - 2, 3)
        field = taps[
            pl.ds(pl.multiple_of(b * CHANNELS, CHANNELS), CHANNELS),
            pl.ds(pl.multiple_of(a * 128, 128), 1024),
        ]
        grads[t] = against(ghid[...], field).astype(BF16)
        core_copy(t).start()

    def x_first(j):
        return j % 2 == 1 or j == SLICES - 1

    def at(axis_x, k):
        return device(z, at_x(k), y, core) if axis_x else device(z, x, at_y(k), core)

    def s1_copy(j, k):
        src = half.at[j, at_x(k)] if x_first(j) else half.at[j, :, at_y(k)]
        return remote(src, in_1.at[j, k - 1], s1_sems, 3 * j + k - 1, at(x_first(j), k))

    def s2_copy(j, k):
        src = mid.at[j, at_y(k) if x_first(j) else at_x(k)]
        return remote(src, in_2.at[j, k - 1], s2_sems, 3 * j + k - 1, at(not x_first(j), k))

    def z_copy(k):
        to = at_z(k)
        return remote(
            sum_f.at[lax.rem(to, 7)], in_z.at[k - 1], z_sems, k - 1, device(to, x, y, core)
        )

    def to_owner(k, act):
        pl.when(at_z(k) < 7)(lambda: act(k))

    def from_owner(k, act):
        pl.when(lax.rem(z + 8 - k, 8) < 7)(lambda: act(k))

    def across_cores(j, begin, end):
        each(end, lambda t: core_copy(t).wait_recv(), begin)

        def add(u):
            unit = 16 * j + u
            t, i = lax.div(unit, 10), lax.rem(unit, 10)
            half[j, lax.div(u, 4), lax.rem(u, 4)] = (
                grads[t, rows16(core * 10 + i)].astype(F32) + in_core[t, rows16(i)].astype(F32)
            ).astype(BF16)

        each(min(16, TAPS * 10 - 16 * j), add, 0)
        each(4, lambda k: s1_copy(j, k).start())

    def across_first(j):
        each(4, lambda k: s1_copy(j, k).wait_recv())
        own = half[j, x] if x_first(j) else half[j, :, y]
        mid[j] = total_of(4, own, lambda k: in_1[j, k - 1]).astype(BF16)
        each(4, lambda k: s2_copy(j, k).start())

    def across_second(j):
        each(4, lambda k: s2_copy(j, k).wait_recv())
        own = mid[j, y if x_first(j) else x]
        sum_f[j] = total_of(4, own, lambda k: in_2[j, k - 1]).astype(BF16)
        pl.when(z != j)(lambda: z_copy(lax.rem(j + 8 - z, 8)).start())

    half[SLICES - 1, 3, pl.ds(2, 2)] = jnp.zeros((2, 16, CHANNELS), BF16)
    pick = Pick(img, row, s_all, s_give, s_got, s_img_sems, s_pair_sems)
    each(3, tap, 2)
    pick.start(row_sum.total().astype(BF16))
    across_cores(0, 0, 2)
    each(5, tap, 3)
    across_cores(1, 2, 4)
    each(6, tap, 5)
    across_cores(2, 4, 5)
    each(8, tap, 6)
    across_cores(3, 5, 7)
    each(9, tap, 8)
    across_cores(4, 7, 8)
    across_first(0)
    each(11, tap, 9)
    across_cores(5, 8, 10)
    across_cores(6, 10, 11)
    across_first(1)
    across_first(2)
    across_second(0)

    pick.relay(group_ref[other])
    across_first(3)
    across_second(1)
    s_image[lax.rem(row, 2), rows16(lax.div(row, 2))] = pick.result(group_ref[img])
    share = Gather(
        ROWS, row, lambda j: (img, j),
        lambda j: s_image.at[lax.rem(j, 2), rows16(lax.div(j, 2))], s_row_sems,
    )
    share.start()
    across_first(4)
    across_second(2)
    across_first(5)
    across_second(3)
    across_first(6)
    across_second(4)

    share.wait()
    features = cond.shape[1]
    for side in range(2):
        k_part[
            pl.ds(0, features // 16), :, side * CHANNELS : (side + 1) * CHANNELS
        ] = (
            lax.dot_general(
                cond[...], s_image[side], (((0,), (0,)), ((), ())), preferred_element_type=F32
            )
            .astype(BF16)
            .reshape(features // 16, 16, CHANNELS)
        )
    k_part[pl.ds(features // 16, 4)] = jnp.zeros((4, 16, 2 * CHANNELS), BF16)

    def kc_copy():
        return remote(k_part.at[pl.ds((1 - core) * 28, 28)], k_core, kc_sems, 0, partner)

    kc_copy().start()
    across_second(5)
    across_second(6)

    def kx1_copy():
        return remote(k_half.at[pl.ds((1 - low) * 7, 7)], k_low1, kx1_sems, 0, across)

    def kz1_copy(k):
        to = at_z(k)
        return remote(
            k_sum1.at[lax.rem(to, 7)], k_z1.at[k - 1], kz1_sems, k - 1, device(to, x, y, core)
        )

    def kz2_copy(k):
        to = at_z(k)
        return remote(
            k_half.at[pl.ds(14 + 2 * lax.rem(to, 7), 2)], k_z2.at[k - 1], kz2_sems, k - 1,
            device(to, x, y, core),
        )

    def kx2_copy():
        return remote(k_sum2.at[1 - low], k_low2, kx2_sems, 0, across)

    kc_copy().wait_recv()

    def add_kc(j):
        k_half[j] = (k_part[core * 28 + j].astype(F32) + k_core[j].astype(F32)).astype(BF16)

    each(28, add_kc, 14)
    each(8, lambda k: to_owner(k, lambda i: kz2_copy(i).start()))
    each(14, add_kc, 0)
    kx1_copy().start()

    zi = lax.rem(z, 7)

    @pl.when(z < 7)
    def _():
        each(8, lambda k: z_copy(k).wait_recv())
        done = total_of(8, sum_f[zi], lambda k: in_z[k - 1]) * weight_scale
        final[core, zi, x, y] = done.astype(BF16)

    def gz_copy(k):
        mine = final.at[core, zi, x, y]
        return remote(mine, mine, gz_sems, k - 1, device(at_z(k), x, y, core))

    @pl.when(z < 7)
    def _():
        each(8, lambda k: gz_copy(k).start())

    gcond = against(jnp.concatenate([s_image[0], s_image[1]], axis=1), kvw_ref[...]).astype(BF16)
    spot = lax.broadcasted_iota(jnp.int32, (hidden_ref.shape[0], SLOTS), 0)
    slot = lax.broadcasted_iota(jnp.int32, (hidden_ref.shape[0], SLOTS), 1) + slot_ref[0]
    ghidden_ref[...] = matmul((spot == slot).astype(BF16), gcond).astype(BF16)

    kx1_copy().wait_recv()

    def add_kx1(j):
        k_sum1[j] = (k_half[low * 7 + j].astype(F32) + k_low1[j].astype(F32)).astype(BF16)

    each(7, add_kx1, 0)
    each(8, lambda k: to_owner(k, lambda i: kz1_copy(i).start()))

    each(5, unflatten, 0)

    def g1_copy(j, k):
        mine = final.at[core, j, x, y]
        return remote(mine, mine, g1_sems, 3 * j + k - 1, at(not x_first(j), k))

    def g2_copy(j, k):
        mine = final.at[core, j, x] if x_first(j) else final.at[core, j, :, y]
        return remote(mine, mine, g2_sems, 3 * j + k - 1, at(x_first(j), k))

    def core_pass(j, k):
        mine = (
            final.at[core, j, lax.rem(x + 4 - k, 4)]
            if x_first(j)
            else final.at[core, j, :, lax.rem(y + 4 - k, 4)]
        )
        return remote(mine, mine, gcore_sems, 4 * j + k, partner)

    def spread_second(j):
        @pl.when(z != j)
        def _():
            gz_copy(lax.rem(z + 8 - j, 8)).wait_recv()

        each(4, lambda k: g1_copy(j, k).start())

    def spread_first(j):
        each(4, lambda k: g1_copy(j, k).wait_recv())
        each(4, lambda k: g2_copy(j, k).start())
        core_pass(j, 0).start()

    def spread_core(j):
        def go(k):
            g2_copy(j, k).wait_recv()
            core_pass(j, k).start()

        each(4, go)

    for j in range(SLICES):
        spread_second(j)

    @pl.when(z < 7)
    def _():
        each(8, lambda k: kz2_copy(k).wait_recv())
        own = k_half[pl.ds(14 + 2 * zi, 2)]
        k_sum2[...] = total_of(8, own, lambda k: k_z2[k - 1]).astype(BF16)
        kx2_copy().start()

    for j in range(SLICES):
        spread_first(j)

    def kgz1_copy(k):
        mine = k_final.at[core, low * 7 + zi]
        return remote(mine, mine, kgz1_sems, k - 1, device(at_z(k), x, y, core))

    def kgx1_copy():
        mine = k_final.at[core, pl.ds(low * 7, 7)]
        return remote(mine, mine, kgx1_sems, 0, across)

    def kgx2_copy():
        mine = k_final.at[core, 14 + 2 * zi + low]
        return remote(mine, mine, kgx2_sems, 0, across)

    def kgz2_copy(k):
        mine = k_final.at[core, pl.ds(14 + 2 * zi, 2)]
        return remote(mine, mine, kgz2_sems, k - 1, device(at_z(k), x, y, core))

    @pl.when(z < 7)
    def _():
        kx2_copy().wait_recv()
        done = (k_sum2[low].astype(F32) + k_low2[...].astype(F32)) * kv_scale
        k_final[core, 14 + 2 * zi + low] = done.astype(BF16)
        kgx2_copy().start()
        each(8, lambda k: kz1_copy(k).wait_recv())
        done = total_of(8, k_sum1[zi], lambda k: k_z1[k - 1]) * kv_scale
        k_final[core, low * 7 + zi] = done.astype(BF16)
        each(8, lambda k: kgz1_copy(k).start())
        kgx2_copy().wait_recv()
        each(8, lambda k: kgz2_copy(k).start())

    for j in range(0, 3):
        spread_core(j)
    each(8, lambda k: from_owner(k, lambda i: kgz1_copy(i).wait_recv()))
    kgx1_copy().start()

    def kgc_copy(k):
        begin, count = ((low * 7, 7), (14, 7), (21, 7), ((1 - low) * 7, 7))[k]
        mine = k_final.at[core, pl.ds(begin, count)]
        return remote(mine, mine, kgc_sems, k, partner)

    kgc_copy(0).start()
    for j in range(3, SLICES):
        spread_core(j)
    each(8, lambda k: from_owner(k, lambda i: kgz2_copy(i).wait_recv()))
    kgc_copy(1).start()
    kgc_copy(2).start()
    kgx1_copy().wait_recv()
    kgc_copy(3).start()

    for j in range(SLICES):
        each(4, lambda k, j=j: core_pass(j, k).wait_recv(), 0)

    for t in range(TAPS):
        target, base = ((query_ref, 0), (out_ref, 0))[t] if t < 2 else (res_ref, (t - 2) * CHANNELS)
        for c in range(2):
            for i in range(10):
                j, rest = divmod(t * 10 + i, 16)
                target[pl.ds(base + c * 160 + i * 16, 16)] = final[c, j, rest // 4, rest % 4]
    for k in range(4):
        kgc_copy(k).wait_recv()
    for unit in range(52):
        kvout_ref[pl.ds(16 * unit, 16)] = k_final[unit // 28, unit % 28]

    pl.when(below)(lambda: halo_up().wait_send())
    pl.when(above)(lambda: halo_down().wait_send())
    for one in (f_sum, f_pick, f_share, row_sum, pick, share):
        one.finish()
    each(TAPS, lambda t: core_copy(t).wait_send(), 0)
    for j in range(SLICES):
        for copy in (s1_copy, s2_copy, g1_copy, g2_copy):
            each(4, lambda k, copy=copy, j=j: copy(j, k).wait_send())
        each(4, lambda k, j=j: core_pass(j, k).wait_send(), 0)
    each(8, lambda k: to_owner(k, lambda i: z_copy(i).wait_send()))
    each(8, lambda k: to_owner(k, lambda i: kz1_copy(i).wait_send()))
    each(8, lambda k: to_owner(k, lambda i: kz2_copy(i).wait_send()))

    @pl.when(z < 7)
    def _():
        for copy in (gz_copy, kgz1_copy, kgz2_copy):
            each(8, lambda k, copy=copy: copy(k).wait_send())
        kx2_copy().wait_send()
        kgx2_copy().wait_send()

    kc_copy().wait_send()
    kx1_copy().wait_send()
    kgx1_copy().wait_send()
    for k in range(4):
        kgc_copy(k).wait_send()


def finish_kernel(*refs):
    count = (len(refs) - 1) // 3
    sems = refs[-1]
    loads = [pltpu.make_async_copy(refs[i], refs[2 * count + i], sems.at[0, i]) for i in range(count)]
    stores = [pltpu.make_async_copy(refs[2 * count + i], refs[count + i], sems.at[1, i]) for i in range(count)]
    for load in loads:
        load.start()
    for load, store in zip(loads, stores):
        load.wait()
        store.start()
    for store in stores:
        store.wait()


def finish(arrays):
    anywhere = pl.BlockSpec(memory_space=pl.ANY)
    return pl.pallas_call(
        finish_kernel,
        out_shape=tuple(jax.ShapeDtypeStruct(a.shape, a.dtype) for a in arrays),
        in_specs=[anywhere] * len(arrays),
        out_specs=(anywhere,) * len(arrays),
        scratch_shapes=[pltpu.VMEM(a.shape, a.dtype) for a in arrays]
        + [pltpu.SemaphoreType.DMA((2, len(arrays)))],
        compiler_params=pltpu.CompilerParams(vmem_limit_bytes=32 * 2**20),
        name="finish",
    )(*arrays)


def shards(
    llm_hidden,
    slot_start,
    image_group,
    timesteps,
    latents,
    noise,
    kv_weight,
    in_weight,
    res_weight,
    query_weight,
    out_weight,
    cotangent,
):
    width, features = CHANNELS, llm_hidden.shape[1]
    frequency = jnp.exp(-math.log(10000.0) * jnp.arange(width // 2, dtype=F32) / (width // 2))
    angles = timesteps[0].astype(F32) * frequency
    emb = jnp.concatenate([jnp.cos(angles), jnp.sin(angles)])[:, None]
    in_matrix = jnp.pad(in_weight.transpose(2, 0, 1, 3), ((0, 0), (0, 0), (0, 0), (0, 4)))
    vmem, smem = pl.BlockSpec(memory_space=pltpu.VMEM), pl.BlockSpec(memory_space=pltpu.SMEM)
    anywhere = pl.BlockSpec(memory_space=pl.ANY)
    dma = lambda n: pltpu.SemaphoreType.DMA((2, n))
    low = lambda *shape: pltpu.VMEM(shape, BF16)
    field, square = low(width, 1024), low(width, width)
    out = lambda *shape: jax.ShapeDtypeStruct(shape, BF16)
    block, res, query, projection, grad_hidden, grad_kv_weight = pl.pallas_call(
        functools.partial(
            kernel,
            weight_scale=(IMGS * ROWS * 1024) ** (-0.5),
            kv_scale=(IMGS * SLOTS) ** (-0.5),
        ),
        out_shape=(
            out(width, 8, 128), out(9 * width, width), out(width, width), out(width, width),
            out(*llm_hidden.shape), out(*kv_weight.shape),
        ),
        in_specs=[smem] * 3 + [vmem] * 8 + [anywhere] * 2,
        out_specs=(vmem,) * 6,
        scratch_shapes=[
            low(9, width, width), low(width, 8, 128), pltpu.SemaphoreType.DMA((2,)),
            pltpu.VMEM((64, 8, 128), F32), field, field,
            pltpu.VMEM((4, 8, 128), F32), pltpu.VMEM((12, 8, 128), F32),
            low(SLOTS, features), pltpu.VMEM((2, SLOTS, width), F32),
            pltpu.VMEM((ROWS - 1, 16, width), F32), low(IMGS // 2, 16, width),
            low(16, width), low(16, width), low(2, SLOTS, width),
            low(3, width, 3 * width), square, square,
            low(3 * width, 1280), pltpu.VMEM((width, 1280), F32),
            field, field, field, field, field, field, field, field, square, square, square, square,
            low(2, SLOTS, width), low(ROWS - 1, 16, width), low(IMGS // 2, 16, width),
            low(16, width), low(16, width), low(2, SLOTS, width),
            low(TAPS, width, width), low(TAPS, 160, width), low(SLICES, 4, 4, 16, width),
            low(SLICES, 3, 4, 16, width), low(SLICES, 4, 16, width), low(SLICES, 3, 16, width),
            low(SLICES, 16, width), low(7, 16, width), low(2, SLICES, 4, 4, 16, width),
            low(56, 16, 2 * width), low(28, 16, 2 * width), low(28, 16, 2 * width),
            low(7, 16, 2 * width), low(7, 16, 2 * width), low(7, 16, 2 * width),
            low(2, 16, 2 * width), low(7, 2, 16, 2 * width), low(16, 2 * width),
            low(2, 28, 16, 2 * width),
            dma(2), dma(7), dma(15), dma(1), dma(7),
            dma(7), dma(15), dma(1), dma(7),
            dma(TAPS), dma(3 * SLICES), dma(3 * SLICES), dma(7),
            dma(7), dma(3 * SLICES), dma(3 * SLICES), dma(4 * SLICES),
            dma(1), dma(1), dma(7), dma(1), dma(7),
            dma(1), dma(7), dma(1), dma(7), dma(4),
        ],
        compiler_params=pltpu.CompilerParams(
            collective_id=0, has_side_effects=True, vmem_limit_bytes=60 * 2**20
        ),
        name="block",
    )(
        image_group, slot_start, timesteps, llm_hidden, kv_weight, latents[0], noise[0], emb,
        in_matrix.reshape(width, 72).astype(BF16), query_weight, out_weight,
        res_weight.reshape(9, width, width), cotangent[0],
    )
    query, projection, block, grad_hidden, grad_kv_weight, res = finish(
        (query, projection, block, grad_hidden, grad_kv_weight, res.reshape(3, 3, width, width))
    )
    return block[None], grad_hidden, grad_kv_weight, res, query, projection


def solution(mesh):
    return jax.shard_map(
        shards,
        mesh=mesh,
        in_specs=(
            P("img", "row"),
            P("img"),
            P(),
            P("img"),
            P("img", None, "row", None),
            P("img", None, "row", None),
            P("row", None),
            P(),
            P(),
            P(),
            P(),
            P("img", None, "row", None),
        ),
        out_specs=(P("img", None, "row", None), P("img", "row"), P("row", None), P(), P(), P()),
        check_vma=False,
    )
```

time: 125 us -> 123 us (0.984)
    pallas_call x1, Pallas kernels: 108 us -> 103 us  [shards(): pl.pallas_call(functools.partial(kernel, weight_scale=(IMGS * ROWS * 1024...]
    pallas_call x0 -> x1, Pallas kernels: none -> 3.6 us  [finish(): pl.pallas_call(finish_kernel, out_shape=tuple((jax.ShapeDtypeStruct(a.sha...]
    unnamed x18 -> x14, local copies, waits for them, and re-layouts: 11.5 us -> 10.4 us
where the time goes in v3:
time: 123 us; the launch traced here: 121 us
  Pallas kernels  107 us (87%)
  local copies, waits for them, and re-layouts  12.7 us (10%)
  between operations  1.96 us (2%)
    pallas_call x1, Pallas kernels, shards(): pl.pallas_call(functools.partial(kernel, weight_scale=(IMGS * ROWS * 1024...  103 us
    unnamed x14, local copies, waits for them, and re-layouts  10.4 us
    pallas_call x1, Pallas kernels, finish(): pl.pallas_call(finish_kernel, out_shape=tuple((jax.ShapeDtypeStruct(a.sha...  3.6 us

profile of v3, /device:TPU:1, one launch (start us, length us, event | category | flops | bytes accessed | tf_op | source)
XLA Modules:
  0.0 121.5 jit_solution(13666961308831348598)
XLA Ops:
  2.0 0.1 pad_maximum_fusion
  2.1 0.8 pad.4
  2.8 0.7 copy.23.inw_ref
  3.6 0.8 broadcast_in_dim.8.emb_ref
  4.3 2.2 %copy.21.hidden_ref = bf16[512,832]{1,0:T(8,128)(2,1)} copy(bf16[512,832]{0,1:T(8,128)(2,1)} %param.12) | data formatting | bytes 1703936 | tf_op args[0]
  6.5 103.0 %block.1 = (bf16[320,8,128]{2,1,0:T(8,128)(2,1)}, bf16[2880,320]{1,0:T(8,128)(2,1)}, bf16[320,320]{1,0:T(8,128)(2,1)}, bf16[320,320]{1,0:T(8,128)(2,1)}, bf16[51...) custom-call(s32[32]{0:T(128)} %group_ref.1, s32[1]{0:T(128)S(6)} %copy.25.slot_ref, s32[1]{0:T(128)S(6)} %copy.26.time_ref, ...), custom_call_target="tpu_custom_call" | custom-call | tf_op jit(solution)/shard_map/block/pallas_call | solution.py:764
  109.6 0.0 copy-start
  109.6 1.6 %copy-done = bf16[2880,320]{1,0:T(8,128)(2,1)S(1)} copy-done((bf16[2880,320]{1,0:T(8,128)(2,1)S(1)}, bf16[2880,320]{1,0:T(8,128)(2,1)}, u32[]{:S(2)}) %copy-start) | copy-done | bytes 1843224
  111.2 0.0 copy-start.1
  111.2 1.2 %copy-done.1 = bf16[832,640]{1,0:T(8,128)(2,1)S(1)} copy-done((bf16[832,640]{1,0:T(8,128)(2,1)S(1)}, bf16[832,640]{1,0:T(8,128)(2,1)}, u32[]{:S(2)}) %copy-start.1) | copy-done | bytes 1064984
  112.5 0.0 copy-start.2
  112.5 1.2 copy-done.2
  113.6 0.0 copy-start.3
  113.6 1.1 copy-done.3
  114.7 0.0 copy-start.4
  114.7 0.9 copy-done.4
  115.7 0.0 copy-start.5
  115.7 0.9 copy-done.5
  116.6 3.6 %finish.1 = (bf16[320,320]{1,0:T(8,128)(2,1)}, bf16[320,320]{1,0:T(8,128)(2,1)}, bf16[320,8,128]{2,1,0:T(8,128)(2,1)}, bf16[512,832]{1,0:T(8,128)(2,1)S(1)}, bf1...) custom-call(bf16[320,320]{1,0:T(8,128)(2,1)S(1)} %copy-done.4, bf16[320,320]{1,0:T(8,128)(2,1)S(1)} %copy-done.5, ...), custom_call_target="tpu_custom_call" | custom-call | tf_op jit(solution)/shard_map/finish/pallas_call | solution.py:727
  120.2 1.2 %copy.24 = bf16[512,832]{0,1:T(8,128)(2,1)} copy(bf16[512,832]{1,0:T(8,128)(2,1)S(1)} %get-tuple-element.37) | data formatting | bytes 1703936
  (1 shorter events, 0.0 us)
Async XLA Ops:
  109.6 1.6 %copy-start = (bf16[2880,320]{1,0:T(8,128)(2,1)S(1)}, bf16[2880,320]{1,0:T(8,128)(2,1)}, u32[]{:S(2)}) copy-start(bf16[2880,320]{1,0:T(8,128)(2,1)} %get-tuple-element.23) | copy-start | bytes 5529604
  111.2 1.2 %copy-start.1 = (bf16[832,640]{1,0:T(8,128)(2,1)S(1)}, bf16[832,640]{1,0:T(8,128)(2,1)}, u32[]{:S(2)}) copy-start(bf16[832,640]{1,0:T(8,128)(2,1)} %get-tuple-element.22.refs_4_) | copy-start | bytes 3194884
  112.5 1.2 copy-start.2
  113.6 1.1 copy-start.3
  114.7 0.9 copy-start.4
  115.7 0.9 copy-start.5

commit v4 on v3

--- a/solution.py
+++ b/solution.py
@@ -160,6 +160,10 @@
     return lax.dot_general(left, right, (((1,), (1,)), ((), ())), preferred_element_type=F32)
 
 
+def against_first(left, right):
+    return lax.dot_general(left, right, (((0,), (0,)), ((), ())), preferred_element_type=F32)
+
+
 def shifted(field, step):
     lane = lax.broadcasted_iota(jnp.int32, (field.shape[0], 128), 1)
     edge = 127 if step > 0 else 0
@@ -190,7 +194,7 @@
     group_ref, slot_ref, time_ref,
     hidden_ref, kvw_ref, latent_ref, noise_ref, emb_ref, inw_ref, qw_ref, ow_ref, resw_hbm, up_hbm,
     block3_ref, res_ref, query_ref, out_ref, ghidden_ref, kvout_ref,
-    resw_ref, up3_ref, load_sems, turn, up_ref, block_ref,
+    resw_ref, up3_ref, load_sems, inw_f, inw_t, turn, up_ref, block_ref,
     noisy, band, cond, part, f_inbox, f_all, f_give, f_got, f_kv, wcat, qw_t, ow_t, taps, first,
     hid, query, att, prob, gatt, gscore, gquery, ghid, bk, bk_t, bv, bv_t,
     gkv, s_inbox, s_all, s_give, s_got, s_image,
@@ -228,10 +232,12 @@
     def at_z(k):
         return lax.rem(z + k, 8)
 
-    token = lax.broadcasted_iota(jnp.int32, (SLOTS, hidden_ref.shape[0]), 1)
-    wanted = lax.broadcasted_iota(jnp.int32, (SLOTS, hidden_ref.shape[0]), 0) + slot_ref[0]
-    cond[...] = matmul((token == wanted).astype(BF16), hidden_ref[...]).astype(BF16)
-    product = matmul(cond[...], kvw_ref[...])
+    tokens = hidden_ref.shape[1]
+    token = lax.broadcasted_iota(jnp.int32, (SLOTS, tokens), 1)
+    wanted = lax.broadcasted_iota(jnp.int32, (SLOTS, tokens), 0) + slot_ref[0]
+    pick_rows = (token == wanted).astype(BF16)
+    cond[...] = against(hidden_ref[...], pick_rows).astype(BF16)
+    product = against_first(cond[...], kvw_ref[...])
     part[0] = product[:, :CHANNELS]
     part[1] = product[:, CHANNELS:]
 
@@ -262,6 +268,10 @@
     f_sum = RowSum(img, row, part, f_inbox, f_sum_sems)
     f_sum.start()
 
+    inw_f[...] = jnp.zeros_like(inw_f)
+    for t in range(9):
+        inw_f[pl.ds(8 * t, 4)] = inw_ref[t].astype(F32)
+    inw_t[...] = inw_f[...].T.astype(BF16)
     loads[0].wait()
     for a in range(3):
         for b in range(3):
@@ -291,7 +301,7 @@
                 pieces += [shifted(n, -1), n, shifted(n, 1)]
             fields.append(jnp.concatenate(pieces, axis=0))
         field = jnp.concatenate(fields, axis=1).astype(BF16)
-        value = matmul(inw_ref[...], field)
+        value = matmul(inw_t[...], field)
         lanes = pl.ds(pl.multiple_of(j * 256, 256), 256)
         first[:, lanes] = value
         v = value + emb_ref[...]
@@ -403,7 +413,7 @@
         core_copy(t).start()
 
     def x_first(j):
-        return j % 2 == 1 or j == SLICES - 1
+        return j % 2 == 1
 
     def at(axis_x, k):
         return device(z, at_x(k), y, core) if axis_x else device(z, x, at_y(k), core)
@@ -470,46 +480,7 @@
     each(11, tap, 9)
     across_cores(5, 8, 10)
     across_cores(6, 10, 11)
-    across_first(1)
-    across_first(2)
-    across_second(0)
-
-    pick.relay(group_ref[other])
-    across_first(3)
-    across_second(1)
-    s_image[lax.rem(row, 2), rows16(lax.div(row, 2))] = pick.result(group_ref[img])
-    share = Gather(
-        ROWS, row, lambda j: (img, j),
-        lambda j: s_image.at[lax.rem(j, 2), rows16(lax.div(j, 2))], s_row_sems,
-    )
-    share.start()
-    across_first(4)
-    across_second(2)
-    across_first(5)
-    across_second(3)
-    across_first(6)
-    across_second(4)
-
-    share.wait()
-    features = cond.shape[1]
-    for side in range(2):
-        k_part[
-            pl.ds(0, features // 16), :, side * CHANNELS : (side + 1) * CHANNELS
-        ] = (
-            lax.dot_general(
-                cond[...], s_image[side], (((0,), (0,)), ((), ())), preferred_element_type=F32
-            )
-            .astype(BF16)
-            .reshape(features // 16, 16, CHANNELS)
-        )
-    k_part[pl.ds(features // 16, 4)] = jnp.zeros((4, 16, 2 * CHANNELS), BF16)
-
-    def kc_copy():
-        return remote(k_part.at[pl.ds((1 - core) * 28, 28)], k_core, kc_sems, 0, partner)
-
-    kc_copy().start()
-    across_second(5)
-    across_second(6)
+    zi = lax.rem(z, 7)
 
     def kx1_copy():
         return remote(k_half.at[pl.ds((1 - low) * 7, 7)], k_low1, kx1_sems, 0, across)
@@ -529,47 +500,6 @@
 
     def kx2_copy():
         return remote(k_sum2.at[1 - low], k_low2, kx2_sems, 0, across)
-
-    kc_copy().wait_recv()
-
-    def add_kc(j):
-        k_half[j] = (k_part[core * 28 + j].astype(F32) + k_core[j].astype(F32)).astype(BF16)
-
-    each(28, add_kc, 14)
-    each(8, lambda k: to_owner(k, lambda i: kz2_copy(i).start()))
-    each(14, add_kc, 0)
-    kx1_copy().start()
-
-    zi = lax.rem(z, 7)
-
-    @pl.when(z < 7)
-    def _():
-        each(8, lambda k: z_copy(k).wait_recv())
-        done = total_of(8, sum_f[zi], lambda k: in_z[k - 1]) * weight_scale
-        final[core, zi, x, y] = done.astype(BF16)
-
-    def gz_copy(k):
-        mine = final.at[core, zi, x, y]
-        return remote(mine, mine, gz_sems, k - 1, device(at_z(k), x, y, core))
-
-    @pl.when(z < 7)
-    def _():
-        each(8, lambda k: gz_copy(k).start())
-
-    gcond = against(jnp.concatenate([s_image[0], s_image[1]], axis=1), kvw_ref[...]).astype(BF16)
-    spot = lax.broadcasted_iota(jnp.int32, (hidden_ref.shape[0], SLOTS), 0)
-    slot = lax.broadcasted_iota(jnp.int32, (hidden_ref.shape[0], SLOTS), 1) + slot_ref[0]
-    ghidden_ref[...] = matmul((spot == slot).astype(BF16), gcond).astype(BF16)
-
-    kx1_copy().wait_recv()
-
-    def add_kx1(j):
-        k_sum1[j] = (k_half[low * 7 + j].astype(F32) + k_low1[j].astype(F32)).astype(BF16)
-
-    each(7, add_kx1, 0)
-    each(8, lambda k: to_owner(k, lambda i: kz1_copy(i).start()))
-
-    each(5, unflatten, 0)
 
     def g1_copy(j, k):
         mine = final.at[core, j, x, y]
@@ -606,8 +536,92 @@
 
         each(4, go)
 
-    for j in range(SLICES):
-        spread_second(j)
+    def kgz1_copy(k):
+        mine = k_final.at[core, low * 7 + zi]
+        return remote(mine, mine, kgz1_sems, k - 1, device(at_z(k), x, y, core))
+
+    def kgx1_copy():
+        mine = k_final.at[core, pl.ds(low * 7, 7)]
+        return remote(mine, mine, kgx1_sems, 0, across)
+
+    def kgx2_copy():
+        mine = k_final.at[core, 14 + 2 * zi + low]
+        return remote(mine, mine, kgx2_sems, 0, across)
+
+    def kgz2_copy(k):
+        mine = k_final.at[core, pl.ds(14 + 2 * zi, 2)]
+        return remote(mine, mine, kgz2_sems, k - 1, device(at_z(k), x, y, core))
+
+    def kgc_copy(k):
+        begin, count = ((low * 7, 7), (14, 7), (21, 7), ((1 - low) * 7, 7))[k]
+        mine = k_final.at[core, pl.ds(begin, count)]
+        return remote(mine, mine, kgc_sems, k, partner)
+
+    pick.relay(group_ref[other])
+    across_first(1)
+    s_image[lax.rem(row, 2), rows16(lax.div(row, 2))] = pick.result(group_ref[img])
+    share = Gather(
+        ROWS, row, lambda j: (img, j),
+        lambda j: s_image.at[lax.rem(j, 2), rows16(lax.div(j, 2))], s_row_sems,
+    )
+    share.start()
+    across_first(2)
+    across_second(0)
+    across_first(3)
+    across_second(1)
+    share.wait()
+    features = cond.shape[0]
+    for side in range(2):
+        k_part[
+            pl.ds(0, features // 16), :, side * CHANNELS : (side + 1) * CHANNELS
+        ] = (
+            matmul(cond[...], s_image[side]).astype(BF16).reshape(features // 16, 16, CHANNELS)
+        )
+    k_part[pl.ds(features // 16, 4)] = jnp.zeros((4, 16, 2 * CHANNELS), BF16)
+
+    def kc_copy():
+        return remote(k_part.at[pl.ds((1 - core) * 28, 28)], k_core, kc_sems, 0, partner)
+
+    kc_copy().start()
+    across_first(4)
+    across_second(2)
+    kc_copy().wait_recv()
+
+    def add_kc(j):
+        k_half[j] = (k_part[core * 28 + j].astype(F32) + k_core[j].astype(F32)).astype(BF16)
+
+    each(28, add_kc, 14)
+    each(8, lambda k: to_owner(k, lambda i: kz2_copy(i).start()))
+    each(14, add_kc, 0)
+    kx1_copy().start()
+
+    across_first(5)
+    across_second(3)
+    kx1_copy().wait_recv()
+
+    def add_kx1(j):
+        k_sum1[j] = (k_half[low * 7 + j].astype(F32) + k_low1[j].astype(F32)).astype(BF16)
+
+    each(7, add_kx1, 0)
+    each(8, lambda k: to_owner(k, lambda i: kz1_copy(i).start()))
+
+    across_first(6)
+    across_second(4)
+    across_second(5)
+    across_second(6)
+    @pl.when(z < 7)
+    def _():
+        each(8, lambda k: z_copy(k).wait_recv())
+        done = total_of(8, sum_f[zi], lambda k: in_z[k - 1]) * weight_scale
+        final[core, zi, x, y] = done.astype(BF16)
+
+    def gz_copy(k):
+        mine = final.at[core, zi, x, y]
+        return remote(mine, mine, gz_sems, k - 1, device(at_z(k), x, y, core))
+
+    @pl.when(z < 7)
+    def _():
+        each(8, lambda k: gz_copy(k).start())
 
     @pl.when(z < 7)
     def _():
@@ -616,24 +630,11 @@
         k_sum2[...] = total_of(8, own, lambda k: k_z2[k - 1]).astype(BF16)
         kx2_copy().start()
 
-    for j in range(SLICES):
-        spread_first(j)
-
-    def kgz1_copy(k):
-        mine = k_final.at[core, low * 7 + zi]
-        return remote(mine, mine, kgz1_sems, k - 1, device(at_z(k), x, y, core))
-
-    def kgx1_copy():
-        mine = k_final.at[core, pl.ds(low * 7, 7)]
-        return remote(mine, mine, kgx1_sems, 0, across)
-
-    def kgx2_copy():
-        mine = k_final.at[core, 14 + 2 * zi + low]
-        return remote(mine, mine, kgx2_sems, 0, across)
-
-    def kgz2_copy(k):
-        mine = k_final.at[core, pl.ds(14 + 2 * zi, 2)]
-        return remote(mine, mine, kgz2_sems, k - 1, device(at_z(k), x, y, core))
+    image = jnp.concatenate([s_image[0], s_image[1]], axis=1)
+    gcond = against(kvw_ref[...], image).astype(BF16)
+    spot = lax.broadcasted_iota(jnp.int32, (SLOTS, tokens), 1)
+    slot = lax.broadcasted_iota(jnp.int32, (SLOTS, tokens), 0) + slot_ref[0]
+    ghidden_ref[...] = matmul(gcond, (spot == slot).astype(BF16)).astype(BF16)
 
     @pl.when(z < 7)
     def _():
@@ -648,22 +649,21 @@
         kgx2_copy().wait_recv()
         each(8, lambda k: kgz2_copy(k).start())
 
-    for j in range(0, 3):
-        spread_core(j)
+    each(5, unflatten, 0)
+    for j in range(SLICES):
+        spread_second(j)
+    for j in range(SLICES):
+        spread_first(j)
     each(8, lambda k: from_owner(k, lambda i: kgz1_copy(i).wait_recv()))
     kgx1_copy().start()
-
-    def kgc_copy(k):
-        begin, count = ((low * 7, 7), (14, 7), (21, 7), ((1 - low) * 7, 7))[k]
-        mine = k_final.at[core, pl.ds(begin, count)]
-        return remote(mine, mine, kgc_sems, k, partner)
-
     kgc_copy(0).start()
-    for j in range(3, SLICES):
+    for j in range(0, 4):
         spread_core(j)
     each(8, lambda k: from_owner(k, lambda i: kgz2_copy(i).wait_recv()))
     kgc_copy(1).start()
     kgc_copy(2).start()
+    for j in range(4, SLICES):
+        spread_core(j)
     kgx1_copy().wait_recv()
     kgc_copy(3).start()
 
@@ -731,7 +731,7 @@
         out_specs=(anywhere,) * len(arrays),
         scratch_shapes=[pltpu.VMEM(a.shape, a.dtype) for a in arrays]
         + [pltpu.SemaphoreType.DMA((2, len(arrays)))],
-        compiler_params=pltpu.CompilerParams(vmem_limit_bytes=32 * 2**20),
+        compiler_params=pltpu.CompilerParams(vmem_limit_bytes=62 * 2**20),
         name="finish",
     )(*arrays)
 
@@ -754,7 +754,6 @@
     frequency = jnp.exp(-math.log(10000.0) * jnp.arange(width // 2, dtype=F32) / (width // 2))
     angles = timesteps[0].astype(F32) * frequency
     emb = jnp.concatenate([jnp.cos(angles), jnp.sin(angles)])[:, None]
-    in_matrix = jnp.pad(in_weight.transpose(2, 0, 1, 3), ((0, 0), (0, 0), (0, 0), (0, 4)))
     vmem, smem = pl.BlockSpec(memory_space=pltpu.VMEM), pl.BlockSpec(memory_space=pltpu.SMEM)
     anywhere = pl.BlockSpec(memory_space=pl.ANY)
     dma = lambda n: pltpu.SemaphoreType.DMA((2, n))
@@ -769,15 +768,15 @@
         ),
         out_shape=(
             out(width, 8, 128), out(9 * width, width), out(width, width), out(width, width),
-            out(*llm_hidden.shape), out(*kv_weight.shape),
+            out(features, llm_hidden.shape[0]), out(*kv_weight.shape),
         ),
         in_specs=[smem] * 3 + [vmem] * 8 + [anywhere] * 2,
         out_specs=(vmem,) * 6,
         scratch_shapes=[
             low(9, width, width), low(width, 8, 128), pltpu.SemaphoreType.DMA((2,)),
-            pltpu.VMEM((64, 8, 128), F32), field, field,
+            pltpu.VMEM((72, width), F32), low(width, 72), pltpu.VMEM((64, 8, 128), F32), field, field,
             pltpu.VMEM((4, 8, 128), F32), pltpu.VMEM((12, 8, 128), F32),
-            low(SLOTS, features), pltpu.VMEM((2, SLOTS, width), F32),
+            low(features, SLOTS), pltpu.VMEM((2, SLOTS, width), F32),
             pltpu.VMEM((ROWS - 1, 16, width), F32), low(IMGS // 2, 16, width),
             low(16, width), low(16, width), low(2, SLOTS, width),
             low(3, width, 3 * width), square, square,
@@ -804,14 +803,14 @@
         ),
         name="block",
     )(
-        image_group, slot_start, timesteps, llm_hidden, kv_weight, latents[0], noise[0], emb,
-        in_matrix.reshape(width, 72).astype(BF16), query_weight, out_weight,
+        image_group, slot_start, timesteps, llm_hidden.T, kv_weight, latents[0], noise[0], emb,
+        in_weight.transpose(0, 1, 3, 2).reshape(9, 4, width), query_weight, out_weight,
         res_weight.reshape(9, width, width), cotangent[0],
     )
     query, projection, block, grad_hidden, grad_kv_weight, res = finish(
         (query, projection, block, grad_hidden, grad_kv_weight, res.reshape(3, 3, width, width))
     )
-    return block[None], grad_hidden, grad_kv_weight, res, query, projection
+    return block[None], grad_hidden.T, grad_kv_weight, res, query, projection
 
 
 def solution(mesh):

time: 123 us -> 109 us (0.89)
  local copies, waits for them, and re-layouts: 12.7 us -> 0.78 us
    unnamed x14 -> x0, local copies, waits for them, and re-layouts: 10.4 us -> none
    pallas_call x1, Pallas kernels: 103 us -> 100 us  [shards(): pl.pallas_call(functools.partial(kernel, weight_scale=(IMGS * ROWS * 1024...]
    pallas_call x1, Pallas kernels: 3.6 us -> 5.24 us  [finish(): pl.pallas_call(finish_kernel, out_shape=tuple((jax.ShapeDtypeStruct(a.sha...]
where the time goes in v4:
time: 109 us; the launch traced here: 108 us
  Pallas kernels  106 us (97%)
  between operations  1.94 us (2%)
    pallas_call x1, Pallas kernels, shards(): pl.pallas_call(functools.partial(kernel, weight_scale=(IMGS * ROWS * 1024...  100 us
    pallas_call x1, Pallas kernels, finish(): pl.pallas_call(finish_kernel, out_shape=tuple((jax.ShapeDtypeStruct(a.sha...  5.24 us

profile of v4, /device:TPU:1, one launch (start us, length us, event | category | flops | bytes accessed | tf_op | source)
XLA Modules:
  0.0 108.4 jit_solution(12435393145112218043)
XLA Ops:
  2.0 0.1 pad_maximum_fusion
  2.1 0.8 broadcast_in_dim.8.emb_ref
  2.8 100.4 %block.1 = (bf16[320,8,128]{2,1,0:T(8,128)(2,1)}, bf16[2880,320]{1,0:T(8,128)(2,1)}, bf16[320,320]{1,0:T(8,128)(2,1)}, bf16[320,320]{1,0:T(8,128)(2,1)}, bf16[83...) custom-call(s32[32]{0:T(128)} %group_ref.1, s32[1]{0:T(128)S(6)} %copy.19.slot_ref, s32[1]{0:T(128)S(6)} %copy.20.time_ref, ...), custom_call_target="tpu_custom_call" | custom-call | tf_op jit(solution)/shard_map/block/pallas_call | solution.py:763
  103.2 5.2 %finish.1 = (bf16[320,320]{1,0:T(8,128)(2,1)}, bf16[320,320]{1,0:T(8,128)(2,1)}, bf16[320,8,128]{2,1,0:T(8,128)(2,1)}, bf16[832,512]{1,0:T(8,128)(2,1)}, bf16[83...) custom-call(bf16[320,320]{1,0:T(8,128)(2,1)} %get-tuple-element.18.refs_0_, ...), custom_call_target="tpu_custom_call" | custom-call | tf_op jit(solution)/shard_map/finish/pallas_call | solution.py:727
  (1 shorter events, 0.0 us)

commit v5 on v4

--- a/solution.py
+++ b/solution.py
@@ -65,10 +65,11 @@
     each(ROWS, lambda k: call((img, lax.rem(row + k, ROWS))))
     each(IMGS // 2, lambda k: call((lax.rem(img + 2 * k, IMGS), row)))
     call((img + 1 - 2 * lax.rem(img, 2), row))
+    call((img + 3 - 2 * lax.rem(img, 4), row))
     z, x, y, core = coords(img, row)
     other = 2 * (1 - lax.div(x, 2)) + (1 - lax.rem(x, 2))
     call(device(z, other, y, core))
-    return ROWS - 1 + IMGS // 2 - 1 + 1 + 1
+    return ROWS - 1 + IMGS // 2 - 1 + 1 + 1 + 1
 
 
 class RowSum:
@@ -146,6 +147,20 @@
     def finish(self):
         self.gather.finish()
         self.pair().wait_send()
+
+
+class PickFour(Pick):
+    def relay(self, wanted):
+        self.gather.wait()
+        for m in range(4):
+            self.give[m] = self.everyone[lax.div(wanted(m), 2)]
+        self.pair().start()
+
+    def result(self, wanted, put):
+        self.pair().wait_recv()
+        for m in range(4):
+            own = self.give[m].astype(F32)
+            put(m, jnp.where(lax.rem(wanted(m), 2) == self.core, own, self.got[m].astype(F32)).astype(BF16))
 
 
 def total_of(count, base, piece):
@@ -199,13 +214,13 @@
     hid, query, att, prob, gatt, gscore, gquery, ghid, bk, bk_t, bv, bv_t,
     gkv, s_inbox, s_all, s_give, s_got, s_image,
     grads, in_core, half, in_1, mid, in_2, sum_f, in_z, final,
-    k_part, k_core, k_half, k_low1, k_z1, k_sum1, k_sum2, k_z2, k_low2, k_final,
+    quarters, four_cond, k_quarter, k_z, k_final,
     halo_sems, f_sum_sems, f_img_sems, f_pair_sems, f_row_sems,
     s_sum_sems, s_img_sems, s_pair_sems, s_row_sems,
     core_sems, s1_sems, s2_sems, z_sems,
     gz_sems, g1_sems, g2_sems, gcore_sems,
-    kc_sems, kx1_sems, kz1_sems, kx2_sems, kz2_sems,
-    kgx1_sems, kgz1_sems, kgx2_sems, kgz2_sems, kgc_sems,
+    q_sems, kz_sems,
+    kgz1_sems, kgx1_sems, kgx2_sems, kgz2_sems, kgc_sems,
     *, weight_scale, kv_scale,
 ):
     loads = [
@@ -237,6 +252,13 @@
     wanted = lax.broadcasted_iota(jnp.int32, (SLOTS, tokens), 0) + slot_ref[0]
     pick_rows = (token == wanted).astype(BF16)
     cond[...] = against(hidden_ref[...], pick_rows).astype(BF16)
+    units = cond[...].reshape(cond.shape[0] // 16, 16, SLOTS)
+    for q in range(4):
+        count = min(14, units.shape[0] - 14 * q)
+        quarters[q, pl.ds(0, count)] = units[14 * q : 14 * q + count]
+    quarters[3, pl.ds(10, 4)] = jnp.zeros((4, 16, SLOTS), BF16)
+    member = lax.rem(img, 4)
+    four_cond[member] = quarters[2 * core + low]
     product = against_first(cond[...], kvw_ref[...])
     part[0] = product[:, :CHANNELS]
     part[1] = product[:, CHANNELS:]
@@ -267,6 +289,15 @@
     pl.when(above)(lambda: halo_down().start())
     f_sum = RowSum(img, row, part, f_inbox, f_sum_sems)
     f_sum.start()
+
+    def quarter_copy(k):
+        to = lax.rem(member + k, 4)
+        return remote(
+            quarters.at[2 * lax.rem(to, 2) + lax.div(to, 2)], four_cond.at[member], q_sems, k - 1,
+            (img - member + to, row),
+        )
+
+    each(4, lambda k: quarter_copy(k).start())
 
     inw_f[...] = jnp.zeros_like(inw_f)
     for t in range(9):
@@ -464,7 +495,7 @@
         pl.when(z != j)(lambda: z_copy(lax.rem(j + 8 - z, 8)).start())
 
     half[SLICES - 1, 3, pl.ds(2, 2)] = jnp.zeros((2, 16, CHANNELS), BF16)
-    pick = Pick(img, row, s_all, s_give, s_got, s_img_sems, s_pair_sems)
+    pick = PickFour(img, row, s_all, s_give, s_got, s_img_sems, s_pair_sems)
     each(3, tap, 2)
     pick.start(row_sum.total().astype(BF16))
     across_cores(0, 0, 2)
@@ -482,24 +513,11 @@
     across_cores(6, 10, 11)
     zi = lax.rem(z, 7)
 
-    def kx1_copy():
-        return remote(k_half.at[pl.ds((1 - low) * 7, 7)], k_low1, kx1_sems, 0, across)
-
-    def kz1_copy(k):
+    def kz_copy(k):
         to = at_z(k)
         return remote(
-            k_sum1.at[lax.rem(to, 7)], k_z1.at[k - 1], kz1_sems, k - 1, device(to, x, y, core)
+            k_quarter.at[:, lax.rem(to, 7)], k_z.at[k - 1], kz_sems, k - 1, device(to, x, y, core)
         )
-
-    def kz2_copy(k):
-        to = at_z(k)
-        return remote(
-            k_half.at[pl.ds(14 + 2 * lax.rem(to, 7), 2)], k_z2.at[k - 1], kz2_sems, k - 1,
-            device(to, x, y, core),
-        )
-
-    def kx2_copy():
-        return remote(k_sum2.at[1 - low], k_low2, kx2_sems, 0, across)
 
     def g1_copy(j, k):
         mine = final.at[core, j, x, y]
@@ -537,32 +555,40 @@
         each(4, go)
 
     def kgz1_copy(k):
-        mine = k_final.at[core, low * 7 + zi]
+        mine = k_final.at[core, low, 0, zi]
         return remote(mine, mine, kgz1_sems, k - 1, device(at_z(k), x, y, core))
 
     def kgx1_copy():
-        mine = k_final.at[core, pl.ds(low * 7, 7)]
+        mine = k_final.at[core, low, 0]
         return remote(mine, mine, kgx1_sems, 0, across)
 
     def kgx2_copy():
-        mine = k_final.at[core, 14 + 2 * zi + low]
+        mine = k_final.at[core, low, 1, zi]
         return remote(mine, mine, kgx2_sems, 0, across)
 
     def kgz2_copy(k):
-        mine = k_final.at[core, pl.ds(14 + 2 * zi, 2)]
+        mine = k_final.at[core, :, 1, zi]
         return remote(mine, mine, kgz2_sems, k - 1, device(at_z(k), x, y, core))
 
     def kgc_copy(k):
-        begin, count = ((low * 7, 7), (14, 7), (21, 7), ((1 - low) * 7, 7))[k]
-        mine = k_final.at[core, pl.ds(begin, count)]
+        part_x, turn_of = ((low, 0), (0, 1), (1, 1), (1 - low, 0))[k]
+        mine = k_final.at[core, part_x, turn_of]
         return remote(mine, mine, kgc_sems, k, partner)
 
-    pick.relay(group_ref[other])
+
+    def wanted(m):
+        return group_ref[4 * z + m]
+
+    pick.relay(wanted)
     across_first(1)
-    s_image[lax.rem(row, 2), rows16(lax.div(row, 2))] = pick.result(group_ref[img])
+
+    def put(m, value):
+        s_image[m, lax.rem(row, 2), rows16(lax.div(row, 2))] = value
+
+    pick.result(wanted, put)
     share = Gather(
         ROWS, row, lambda j: (img, j),
-        lambda j: s_image.at[lax.rem(j, 2), rows16(lax.div(j, 2))], s_row_sems,
+        lambda j: s_image.at[:, lax.rem(j, 2), rows16(lax.div(j, 2))], s_row_sems,
     )
     share.start()
     across_first(2)
@@ -570,41 +596,19 @@
     across_first(3)
     across_second(1)
     share.wait()
-    features = cond.shape[0]
+    each(4, lambda k: quarter_copy(k).wait_recv())
     for side in range(2):
-        k_part[
-            pl.ds(0, features // 16), :, side * CHANNELS : (side + 1) * CHANNELS
-        ] = (
-            matmul(cond[...], s_image[side]).astype(BF16).reshape(features // 16, 16, CHANNELS)
+        total = jnp.zeros((224, CHANNELS), F32)
+        for m in range(4):
+            total = total + matmul(four_cond[m].reshape(224, SLOTS), s_image[m, side])
+        k_quarter[:, :, :, side * CHANNELS : (side + 1) * CHANNELS] = total.astype(BF16).reshape(
+            2, 7, 16, CHANNELS
         )
-    k_part[pl.ds(features // 16, 4)] = jnp.zeros((4, 16, 2 * CHANNELS), BF16)
-
-    def kc_copy():
-        return remote(k_part.at[pl.ds((1 - core) * 28, 28)], k_core, kc_sems, 0, partner)
-
-    kc_copy().start()
+    each(8, lambda k: to_owner(k, lambda i: kz_copy(i).start()))
     across_first(4)
     across_second(2)
-    kc_copy().wait_recv()
-
-    def add_kc(j):
-        k_half[j] = (k_part[core * 28 + j].astype(F32) + k_core[j].astype(F32)).astype(BF16)
-
-    each(28, add_kc, 14)
-    each(8, lambda k: to_owner(k, lambda i: kz2_copy(i).start()))
-    each(14, add_kc, 0)
-    kx1_copy().start()
-
     across_first(5)
     across_second(3)
-    kx1_copy().wait_recv()
-
-    def add_kx1(j):
-        k_sum1[j] = (k_half[low * 7 + j].astype(F32) + k_low1[j].astype(F32)).astype(BF16)
-
-    each(7, add_kx1, 0)
-    each(8, lambda k: to_owner(k, lambda i: kz1_copy(i).start()))
-
     across_first(6)
     across_second(4)
     across_second(5)
@@ -625,12 +629,14 @@
 
     @pl.when(z < 7)
     def _():
-        each(8, lambda k: kz2_copy(k).wait_recv())
-        own = k_half[pl.ds(14 + 2 * zi, 2)]
-        k_sum2[...] = total_of(8, own, lambda k: k_z2[k - 1]).astype(BF16)
-        kx2_copy().start()
-
-    image = jnp.concatenate([s_image[0], s_image[1]], axis=1)
+        each(8, lambda k: kz_copy(k).wait_recv())
+        done = (total_of(8, k_quarter[:, zi], lambda k: k_z[k - 1]) * kv_scale).astype(BF16)
+        k_final[core, low, 0, zi] = done[0]
+        k_final[core, low, 1, zi] = done[1]
+        kgx2_copy().start()
+        each(8, lambda k: kgz1_copy(k).start())
+
+    image = jnp.concatenate([s_image[member, 0], s_image[member, 1]], axis=1)
     gcond = against(kvw_ref[...], image).astype(BF16)
     spot = lax.broadcasted_iota(jnp.int32, (SLOTS, tokens), 1)
     slot = lax.broadcasted_iota(jnp.int32, (SLOTS, tokens), 0) + slot_ref[0]
@@ -638,14 +644,6 @@
 
     @pl.when(z < 7)
     def _():
-        kx2_copy().wait_recv()
-        done = (k_sum2[low].astype(F32) + k_low2[...].astype(F32)) * kv_scale
-        k_final[core, 14 + 2 * zi + low] = done.astype(BF16)
-        kgx2_copy().start()
-        each(8, lambda k: kz1_copy(k).wait_recv())
-        done = total_of(8, k_sum1[zi], lambda k: k_z1[k - 1]) * kv_scale
-        k_final[core, low * 7 + zi] = done.astype(BF16)
-        each(8, lambda k: kgz1_copy(k).start())
         kgx2_copy().wait_recv()
         each(8, lambda k: kgz2_copy(k).start())
 
@@ -679,7 +677,8 @@
     for k in range(4):
         kgc_copy(k).wait_recv()
     for unit in range(52):
-        kvout_ref[pl.ds(16 * unit, 16)] = k_final[unit // 28, unit % 28]
+        q, rest = divmod(unit, 14)
+        kvout_ref[pl.ds(16 * unit, 16)] = k_final[q // 2, q % 2, rest // 7, rest % 7]
 
     pl.when(below)(lambda: halo_up().wait_send())
     pl.when(above)(lambda: halo_down().wait_send())
@@ -691,18 +690,15 @@
             each(4, lambda k, copy=copy, j=j: copy(j, k).wait_send())
         each(4, lambda k, j=j: core_pass(j, k).wait_send(), 0)
     each(8, lambda k: to_owner(k, lambda i: z_copy(i).wait_send()))
-    each(8, lambda k: to_owner(k, lambda i: kz1_copy(i).wait_send()))
-    each(8, lambda k: to_owner(k, lambda i: kz2_copy(i).wait_send()))
+    each(8, lambda k: to_owner(k, lambda i: kz_copy(i).wait_send()))
+    each(4, lambda k: quarter_copy(k).wait_send())
 
     @pl.when(z < 7)
     def _():
         for copy in (gz_copy, kgz1_copy, kgz2_copy):
             each(8, lambda k, copy=copy: copy(k).wait_send())
-        kx2_copy().wait_send()
         kgx2_copy().wait_send()
 
-    kc_copy().wait_send()
-    kx1_copy().wait_send()
     kgx1_copy().wait_send()
     for k in range(4):
         kgc_copy(k).wait_send()
@@ -783,20 +779,18 @@
             low(3 * width, 1280), pltpu.VMEM((width, 1280), F32),
             field, field, field, field, field, field, field, field, square, square, square, square,
             low(2, SLOTS, width), low(ROWS - 1, 16, width), low(IMGS // 2, 16, width),
-            low(16, width), low(16, width), low(2, SLOTS, width),
+            low(4, 16, width), low(4, 16, width), low(4, 2, SLOTS, width),
             low(TAPS, width, width), low(TAPS, 160, width), low(SLICES, 4, 4, 16, width),
             low(SLICES, 3, 4, 16, width), low(SLICES, 4, 16, width), low(SLICES, 3, 16, width),
             low(SLICES, 16, width), low(7, 16, width), low(2, SLICES, 4, 4, 16, width),
-            low(56, 16, 2 * width), low(28, 16, 2 * width), low(28, 16, 2 * width),
-            low(7, 16, 2 * width), low(7, 16, 2 * width), low(7, 16, 2 * width),
-            low(2, 16, 2 * width), low(7, 2, 16, 2 * width), low(16, 2 * width),
-            low(2, 28, 16, 2 * width),
+            low(4, 14, 16, SLOTS), low(4, 14, 16, SLOTS), low(2, 7, 16, 2 * width),
+            low(7, 2, 16, 2 * width), low(2, 2, 2, 7, 16, 2 * width),
             dma(2), dma(7), dma(15), dma(1), dma(7),
             dma(7), dma(15), dma(1), dma(7),
             dma(TAPS), dma(3 * SLICES), dma(3 * SLICES), dma(7),
             dma(7), dma(3 * SLICES), dma(3 * SLICES), dma(4 * SLICES),
-            dma(1), dma(1), dma(7), dma(1), dma(7),
-            dma(1), dma(7), dma(1), dma(7), dma(4),
+            dma(3), dma(7),
+            dma(7), dma(1), dma(1), dma(7), dma(4),
         ],
         compiler_params=pltpu.CompilerParams(
             collective_id=0, has_side_effects=True, vmem_limit_bytes=60 * 2**20

time: 109 us -> 107 us (0.982)
  Pallas kernels: 106 us -> 104 us
    pallas_call x1, Pallas kernels: 100 us -> 99.2 us  [shards(): pl.pallas_call(functools.partial(kernel, weight_scale=(IMGS * ROWS * 1024...]
where the time goes in v5:
time: 107 us
  Pallas kernels  104 us (97%)
  between operations  1.94 us (2%)
    pallas_call x1, Pallas kernels, shards(): pl.pallas_call(functools.partial(kernel, weight_scale=(IMGS * ROWS * 1024...  99.2 us
    pallas_call x1, Pallas kernels, finish(): pl.pallas_call(finish_kernel, out_shape=tuple((jax.ShapeDtypeStruct(a.sha...  5.24 us

profile of v5, /device:TPU:1, one launch (start us, length us, event | category | flops | bytes accessed | tf_op | source)
XLA Modules:
  0.0 107.3 jit_solution(13912232536787808914)
XLA Ops:
  2.0 0.1 pad_maximum_fusion
  2.1 0.8 broadcast_in_dim.8.emb_ref
  2.8 99.2 %block.1 = (bf16[320,8,128]{2,1,0:T(8,128)(2,1)}, bf16[2880,320]{1,0:T(8,128)(2,1)}, bf16[320,320]{1,0:T(8,128)(2,1)}, bf16[320,320]{1,0:T(8,128)(2,1)}, bf16[83...) custom-call(s32[32]{0:T(128)} %group_ref.1, s32[1]{0:T(128)S(6)} %copy.19.slot_ref, s32[1]{0:T(128)S(6)} %copy.20.time_ref, ...), custom_call_target="tpu_custom_call" | custom-call | tf_op jit(solution)/shard_map/block/pallas_call | solution.py:759
  102.1 5.2 %finish.1 = (bf16[320,320]{1,0:T(8,128)(2,1)}, bf16[320,320]{1,0:T(8,128)(2,1)}, bf16[320,8,128]{2,1,0:T(8,128)(2,1)}, bf16[832,512]{1,0:T(8,128)(2,1)}, bf16[83...) custom-call(bf16[320,320]{1,0:T(8,128)(2,1)} %get-tuple-element.18.refs_0_, ...), custom_call_target="tpu_custom_call" | custom-call | tf_op jit(solution)/shard_map/finish/pallas_call | solution.py:723
  (1 shorter events, 0.0 us)

commit v6 on v5

--- a/solution.py
+++ b/solution.py
@@ -66,10 +66,11 @@
     each(IMGS // 2, lambda k: call((lax.rem(img + 2 * k, IMGS), row)))
     call((img + 1 - 2 * lax.rem(img, 2), row))
     call((img + 3 - 2 * lax.rem(img, 4), row))
+    each(ROWS, lambda k: call((img + 1 - 2 * lax.rem(img, 2), lax.rem(row + k, ROWS))))
     z, x, y, core = coords(img, row)
     other = 2 * (1 - lax.div(x, 2)) + (1 - lax.rem(x, 2))
     call(device(z, other, y, core))
-    return ROWS - 1 + IMGS // 2 - 1 + 1 + 1 + 1
+    return ROWS - 1 + IMGS // 2 - 1 + 1 + 1 + 1 + ROWS - 1
 
 
 class RowSum:
@@ -210,7 +211,7 @@
     hidden_ref, kvw_ref, latent_ref, noise_ref, emb_ref, inw_ref, qw_ref, ow_ref, resw_hbm, up_hbm,
     block3_ref, res_ref, query_ref, out_ref, ghidden_ref, kvout_ref,
     resw_ref, up3_ref, load_sems, inw_f, inw_t, turn, up_ref, block_ref,
-    noisy, band, cond, part, f_inbox, f_all, f_give, f_got, f_kv, wcat, qw_t, ow_t, taps, first,
+    noisy, band, cond, part, f_inbox, f_all, f_give, f_kv, wcat, qw_t, ow_t, taps, first,
     hid, query, att, prob, gatt, gscore, gquery, ghid, bk, bk_t, bv, bv_t,
     gkv, s_inbox, s_all, s_give, s_got, s_image,
     grads, in_core, half, in_1, mid, in_2, sum_f, in_z, final,
@@ -317,8 +318,12 @@
 
     other = img + 1 - 2 * core
     source, other_source = source_of(img), source_of(other)
-    f_pick = Pick(img, row, f_all, f_give, f_got, f_img_sems, f_pair_sems)
-    f_pick.start(f_sum.total().astype(BF16))
+    half_img = lax.div(img, 2)
+    f_gather = Gather(
+        IMGS // 2, half_img, lambda j: (2 * j + core, row), lambda j: f_all.at[j], f_img_sems
+    )
+    f_all[half_img] = f_sum.total().astype(BF16)
+    f_gather.start()
 
     pl.when(above)(lambda: halo_up().wait_recv())
     pl.when(below)(lambda: halo_down().wait_recv())
@@ -354,15 +359,23 @@
             acc = acc + matmul(wcat[a], taps[:, cells(n, 128 * a)])
         hid[:, cells(n)] = acc.astype(BF16)
 
-    each(2, residual, 0)
-    f_pick.relay(other_source)
-    each(4, residual, 2)
-
-    f_kv[lax.rem(row, 2), rows16(lax.div(row, 2))] = f_pick.result(source)
-    f_share = Gather(
-        ROWS, row, lambda j: (img, j),
-        lambda j: f_kv.at[lax.rem(j, 2), rows16(lax.div(j, 2))], f_row_sems,
-    )
+    each(4, residual, 0)
+
+
+    def band_slot(which, j):
+        return f_kv.at[which, lax.rem(j, 2), rows16(lax.div(j, 2))]
+
+    f_gather.wait()
+    f_kv[0, lax.rem(row, 2), rows16(lax.div(row, 2))] = f_all[lax.div(source, 2)]
+    f_give[...] = f_all[lax.div(other_source, 2)]
+    f_share = Gather(ROWS, row, lambda j: (img, j), lambda j: band_slot(0, j), f_row_sems)
+
+    def f_cross(k):
+        return remote(
+            f_give, band_slot(1, row), f_pair_sems, k, (other, lax.rem(row + k, ROWS))
+        )
+
+    each(ROWS, lambda k: f_cross(k).start(), 0)
     f_share.start()
 
     loads[1].wait()
@@ -387,8 +400,10 @@
 
     each(4, projections, 0)
     f_share.wait()
-    spread(f_kv[0], bk, bk_t)
-    spread(f_kv[1], bv, bv_t)
+    each(ROWS, lambda k: f_cross(k).wait_recv(), 0)
+    same = lax.rem(source, 2) == core
+    for side, (wide, flip) in enumerate(((bk, bk_t), (bv, bv_t))):
+        spread(jnp.where(same, f_kv[0, side].astype(F32), f_kv[1, side].astype(F32)), wide, flip)
 
     def attend(n):
         here = cells(n)
@@ -682,8 +697,9 @@
 
     pl.when(below)(lambda: halo_up().wait_send())
     pl.when(above)(lambda: halo_down().wait_send())
-    for one in (f_sum, f_pick, f_share, row_sum, pick, share):
+    for one in (f_sum, f_gather, f_share, row_sum, pick, share):
         one.finish()
+    each(ROWS, lambda k: f_cross(k).wait_send(), 0)
     each(TAPS, lambda t: core_copy(t).wait_send(), 0)
     for j in range(SLICES):
         for copy in (s1_copy, s2_copy, g1_copy, g2_copy):
@@ -774,7 +790,7 @@
             pltpu.VMEM((4, 8, 128), F32), pltpu.VMEM((12, 8, 128), F32),
             low(features, SLOTS), pltpu.VMEM((2, SLOTS, width), F32),
             pltpu.VMEM((ROWS - 1, 16, width), F32), low(IMGS // 2, 16, width),
-            low(16, width), low(16, width), low(2, SLOTS, width),
+            low(16, width), low(2, 2, SLOTS, width),
             low(3, width, 3 * width), square, square,
             low(3 * width, 1280), pltpu.VMEM((width, 1280), F32),
             field, field, field, field, field, field, field, field, square, square, square, square,
@@ -785,7 +801,7 @@
             low(SLICES, 16, width), low(7, 16, width), low(2, SLICES, 4, 4, 16, width),
             low(4, 14, 16, SLOTS), low(4, 14, 16, SLOTS), low(2, 7, 16, 2 * width),
             low(7, 2, 16, 2 * width), low(2, 2, 2, 7, 16, 2 * width),
-            dma(2), dma(7), dma(15), dma(1), dma(7),
+            dma(2), dma(7), dma(15), dma(ROWS), dma(7),
             dma(7), dma(15), dma(1), dma(7),
             dma(TAPS), dma(3 * SLICES), dma(3 * SLICES), dma(7),
             dma(7), dma(3 * SLICES), dma(3 * SLICES), dma(4 * SLICES),

time: 107 us -> 108 us (level)
  no operation moved by 1% of the time
where the time goes in v6:
time: 108 us
  Pallas kernels  105 us (97%)
  between operations  1.94 us (2%)
    pallas_call x1, Pallas kernels, shards(): pl.pallas_call(functools.partial(kernel, weight_scale=(IMGS * ROWS * 1024...  99.9 us
    pallas_call x1, Pallas kernels, finish(): pl.pallas_call(finish_kernel, out_shape=tuple((jax.ShapeDtypeStruct(a.sha...  5.24 us

profile of v6, /device:TPU:1, one launch (start us, length us, event | category | flops | bytes accessed | tf_op | source)
XLA Modules:
  0.0 108.0 jit_solution(12656746998670956378)
XLA Ops:
  2.0 0.1 pad_maximum_fusion
  2.1 0.8 broadcast_in_dim.8.emb_ref
  2.8 99.9 %block.1 = (bf16[320,8,128]{2,1,0:T(8,128)(2,1)}, bf16[2880,320]{1,0:T(8,128)(2,1)}, bf16[320,320]{1,0:T(8,128)(2,1)}, bf16[320,320]{1,0:T(8,128)(2,1)}, bf16[83...) custom-call(s32[32]{0:T(128)} %group_ref.1, s32[1]{0:T(128)S(6)} %copy.19.slot_ref, s32[1]{0:T(128)S(6)} %copy.20.time_ref, ...), custom_call_target="tpu_custom_call" | custom-call | tf_op jit(solution)/shard_map/block/pallas_call | solution.py:775
  102.7 5.2 %finish.1 = (bf16[320,320]{1,0:T(8,128)(2,1)}, bf16[320,320]{1,0:T(8,128)(2,1)}, bf16[320,8,128]{2,1,0:T(8,128)(2,1)}, bf16[832,512]{1,0:T(8,128)(2,1)}, bf16[83...) custom-call(bf16[320,320]{1,0:T(8,128)(2,1)} %get-tuple-element.18.refs_0_, ...), custom_call_target="tpu_custom_call" | custom-call | tf_op jit(solution)/shard_map/finish/pallas_call | solution.py:739
  (1 shorter events, 0.0 us)

commit v7 on v5

--- a/solution.py
+++ b/solution.py
@@ -704,11 +704,22 @@
         kgc_copy(k).wait_send()
 
 
+FINISH_PARTS = (1, 1, 4, 4, 4, 3)
+
+
 def finish_kernel(*refs):
     count = (len(refs) - 1) // 3
     sems = refs[-1]
-    loads = [pltpu.make_async_copy(refs[i], refs[2 * count + i], sems.at[0, i]) for i in range(count)]
-    stores = [pltpu.make_async_copy(refs[2 * count + i], refs[count + i], sems.at[1, i]) for i in range(count)]
+    loads, stores = [], []
+    for i in range(count):
+        rows = refs[i].shape[0]
+        pieces = FINISH_PARTS[i]
+        for p in range(pieces):
+            here = pl.ds(p * (rows // pieces), rows // pieces)
+            slot = len(loads)
+            held = refs[2 * count + i].at[here]
+            loads.append(pltpu.make_async_copy(refs[i].at[here], held, sems.at[0, slot]))
+            stores.append(pltpu.make_async_copy(held, refs[count + i].at[here], sems.at[1, slot]))
     for load in loads:
         load.start()
     for load, store in zip(loads, stores):
@@ -726,7 +737,7 @@
         in_specs=[anywhere] * len(arrays),
         out_specs=(anywhere,) * len(arrays),
         scratch_shapes=[pltpu.VMEM(a.shape, a.dtype) for a in arrays]
-        + [pltpu.SemaphoreType.DMA((2, len(arrays)))],
+        + [pltpu.SemaphoreType.DMA((2, sum(FINISH_PARTS)))],
         compiler_params=pltpu.CompilerParams(vmem_limit_bytes=62 * 2**20),
         name="finish",
     )(*arrays)

time: 107 us -> 107 us (level)
  no operation moved by 1% of the time
where the time goes in v7:
time: 107 us
  Pallas kernels  104 us (97%)
  between operations  1.94 us (2%)
    pallas_call x1, Pallas kernels, shards(): pl.pallas_call(functools.partial(kernel, weight_scale=(IMGS * ROWS * 1024...  99.2 us
    pallas_call x1, Pallas kernels, finish(): pl.pallas_call(finish_kernel, out_shape=tuple((jax.ShapeDtypeStruct(a.sha...  4.91 us

profile of v7, /device:TPU:1, one launch (start us, length us, event | category | flops | bytes accessed | tf_op | source)
XLA Modules:
  0.0 107.0 jit_solution(3075253693769521201)
XLA Ops:
  2.0 0.1 pad_maximum_fusion
  2.1 0.8 broadcast_in_dim.8.emb_ref
  2.8 99.2 %block.1 = (bf16[320,8,128]{2,1,0:T(8,128)(2,1)}, bf16[2880,320]{1,0:T(8,128)(2,1)}, bf16[320,320]{1,0:T(8,128)(2,1)}, bf16[320,320]{1,0:T(8,128)(2,1)}, bf16[83...) custom-call(s32[32]{0:T(128)} %group_ref.1, s32[1]{0:T(128)S(6)} %copy.19.slot_ref, s32[1]{0:T(128)S(6)} %copy.20.time_ref, ...), custom_call_target="tpu_custom_call" | custom-call | tf_op jit(solution)/shard_map/block/pallas_call | solution.py:770
  102.1 4.9 %finish.1 = (bf16[320,320]{1,0:T(8,128)(2,1)}, bf16[320,320]{1,0:T(8,128)(2,1)}, bf16[320,8,128]{2,1,0:T(8,128)(2,1)}, bf16[832,512]{1,0:T(8,128)(2,1)}, bf16[83...) custom-call(bf16[320,320]{1,0:T(8,128)(2,1)} %get-tuple-element.18.refs_0_, ...), custom_call_target="tpu_custom_call" | custom-call | tf_op jit(solution)/shard_map/finish/pallas_call | solution.py:734
  (1 shorter events, 0.0 us)
